TPU v7x, 512 devices: a whole 4x4x16 slice. The times are simulated.
512 devices in a mesh: lat: 32 (over x, z_lo), lon: 16 (over y, z_hi, core).
Axes of the slice: x: 4, y: 4, z: 16 (z_hi: 2, z_lo: 8; z = z_hi * 8 + z_lo), core: 2. Of those that a mesh axis runs over, the one named last changes fastest.
Arguments:
- thermal_anomaly_field: float32 [16, 1024, 2048], P(None, 'lat', 'lon'), may hold values from -6 to 6
- seawater_salt_anomaly: float32 [16, 1024, 2048], P(None, 'lat', 'lon'), may hold values from -6 to 6
- longitude_flow_speed: float32 [16, 1024, 2048], P(None, 'lat', 'lon'), may hold values from -0.45 to 0.45
- latitude_flow_speed: float32 [16, 1024, 2048], P(None, 'lat', 'lon'), may hold values from -0.45 to 0.45
- marine_profile_flag: int32 [1024, 2048], P('lat', 'lon'), may hold values 0 or 1
- submerged_layer_tally: int32 [1024, 2048], P('lat', 'lon'), may hold values from 1 to 16
Outputs:
- temperature_next: float32 [16, 1024, 2048], P(None, 'lat', 'lon')
- salinity_next: float32 [16, 1024, 2048], P(None, 'lat', 'lon')
- east_next: float32 [16, 1024, 2048], P(None, 'lat', 'lon')
- north_next: float32 [16, 1024, 2048], P(None, 'lat', 'lon')
All inputs are finite; a program needn't handle non-finite values. No bound on the sum of `marine_profile_flag` on one device may be relied on, other than what follows from the above.
Results may differ from a plain program's by a relative error of at most 0.0003.
Values sent between devices are 32-bit elements; how exact they have to be, the bound alone decides.
No kernel may reach another device: no remote copies, remote signals or barrier semaphores. Data moves between devices by JAX's collectives and lax.ppermute only.
A program may use at most 64 MiB of HBM per device.

v0:
```python
import jax
import jax.numpy as jnp
from jax import lax
from jax.sharding import PartitionSpec as P

MIXING = 0.2
VISCOSITY = 0.05
ROTATION = 0.3


def with_halo(cells, sides, width, closed):
    for axis, dim in sides:
        count = lax.axis_size(axis)
        ends = count if closed else count - 1
        head = lax.slice_in_dim(cells, 0, width, axis=dim)
        tail = lax.slice_in_dim(cells, cells.shape[dim] - width, cells.shape[dim], axis=dim)
        cells = jnp.concatenate(
            [
                lax.ppermute(tail, axis, [(i, (i + 1) % count) for i in range(ends)]),
                cells,
                lax.ppermute(head, axis, [((i + 1) % count, i) for i in range(ends)]),
            ],
            axis=dim,
        )
    return cells


def swapped(array, axis, stride):
    return lax.ppermute(array, axis, [(i, i ^ 1 << stride) for i in range(lax.axis_size(axis))])


def row_angles(row_ids, total_rows):
    mirrored = jnp.where(row_ids >= total_rows, 2 * total_rows - 1 - row_ids, row_ids)
    return ROTATION * (2.0 * (mirrored.astype(jnp.float32) + 0.5) / total_rows - 1.0)


def substep(padded, angles):
    planes = padded.shape[0]
    layer_ordinal_index = (planes - 1) // 4
    profile_layer_height = padded[planes - 1]
    ordinal = jnp.arange(layer_ordinal_index, dtype=jnp.float32)[:, None, None]
    wetness = (ordinal < profile_layer_height[None]).astype(jnp.float32)
    heat = padded[:layer_ordinal_index]
    saltiness = padded[layer_ordinal_index : 2 * layer_ordinal_index]
    zonal = padded[2 * layer_ordinal_index : 3 * layer_ordinal_index]
    meridional = padded[3 * layer_ordinal_index : 4 * layer_ordinal_index]
    inside = wetness[:, 1:-1, 1:-1]
    east_face = (
        0.5
        * (zonal[:, 1:-1, :-1] + zonal[:, 1:-1, 1:])
        * (wetness[:, 1:-1, :-1] * wetness[:, 1:-1, 1:])
    )
    north_face = (
        0.5
        * (meridional[:, :-1, 1:-1] + meridional[:, 1:, 1:-1])
        * (wetness[:, :-1, 1:-1] * wetness[:, 1:, 1:-1])
    )

    def transport(quantity):
        across = (
            jnp.maximum(east_face, 0.0) * quantity[:, 1:-1, :-1]
            + jnp.minimum(east_face, 0.0) * quantity[:, 1:-1, 1:]
        )
        upward = (
            jnp.maximum(north_face, 0.0) * quantity[:, :-1, 1:-1]
            + jnp.minimum(north_face, 0.0) * quantity[:, 1:, 1:-1]
        )
        return across[:, :, 1:] - across[:, :, :-1] + (upward[:, 1:, :] - upward[:, :-1, :])

    def mixing(centre):
        vertical = MIXING * (centre[1:] - centre[:-1]) * (inside[1:] * inside[:-1])
        zeroes = jnp.zeros_like(centre[:1])
        return jnp.concatenate([vertical, zeroes], 0) - jnp.concatenate([zeroes, vertical], 0)

    def spread(quantity, centre):
        zonal_part = (quantity[:, 1:-1, 2:] - centre) * wetness[:, 1:-1, 2:] + (
            quantity[:, 1:-1, :-2] - centre
        ) * wetness[:, 1:-1, :-2]
        merid_part = (quantity[:, 2:, 1:-1] - centre) * wetness[:, 2:, 1:-1] + (
            quantity[:, :-2, 1:-1] - centre
        ) * wetness[:, :-2, 1:-1]
        return zonal_part + merid_part

    def tracer(quantity):
        centre = quantity[:, 1:-1, 1:-1]
        return inside * (centre - transport(quantity) + mixing(centre))

    zonal_c = zonal[:, 1:-1, 1:-1]
    merid_c = meridional[:, 1:-1, 1:-1]
    zonal_a = zonal_c - transport(zonal) + VISCOSITY * spread(zonal, zonal_c)
    merid_a = merid_c - transport(meridional) + VISCOSITY * spread(meridional, merid_c)
    cosine = jnp.cos(angles)[None, :, None]
    sine = jnp.sin(angles)[None, :, None]
    zonal_n = inside * (cosine * zonal_a + sine * merid_a)
    merid_n = inside * (cosine * merid_a - sine * zonal_a)
    return jnp.concatenate(
        [tracer(heat), tracer(saltiness), zonal_n, merid_n, profile_layer_height[None, 1:-1, 1:-1]],
        0,
    )


def fold_signs(planes):
    layer_ordinal_index = (planes - 1) // 4
    ordinal = jnp.arange(planes)
    return jnp.where(
        (ordinal >= 2 * layer_ordinal_index) & (ordinal < 4 * layer_ordinal_index), -1.0, 1.0
    ).astype(jnp.float32)[:, None, None]


def extend(marine_condition_bundle, margin):
    local_rows = marine_condition_bundle.shape[1]
    zonal_rim = with_halo(marine_condition_bundle, (("lon", 2),), margin, True)
    complete = with_halo(zonal_rim, (("lat", 1),), margin, False)
    top_strip = zonal_rim[:, local_rows - margin : local_rows, :]
    mirror = top_strip
    for bit_number in range(lax.axis_size("lon").bit_length() - 1):
        mirror = swapped(mirror, "lon", bit_number)
    folded = mirror[:, ::-1, ::-1] * fold_signs(marine_condition_bundle.shape[0])
    at_top = lax.axis_index("lat") == lax.axis_size("lat") - 1
    northern = jnp.where(at_top, folded, complete[:, local_rows + margin :, :])
    return jnp.concatenate([complete[:, : local_rows + margin, :], northern], 1)


def on_device(
    thermal_anomaly_field,
    seawater_salt_anomaly,
    longitude_flow_speed,
    latitude_flow_speed,
    marine_profile_flag,
    submerged_layer_tally,
):
    profile_layer_height = (marine_profile_flag * submerged_layer_tally).astype(jnp.float32)[None]
    marine_condition_bundle = jnp.concatenate(
        [
            thermal_anomaly_field,
            seawater_salt_anomaly,
            longitude_flow_speed,
            latitude_flow_speed,
            profile_layer_height,
        ],
        0,
    )
    local_rows = marine_condition_bundle.shape[1]
    total_rows = local_rows * lax.axis_size("lat")
    first_row = lax.axis_index("lat") * local_rows
    own_rows = first_row + jnp.arange(local_rows, dtype=jnp.int32)
    for repeat in range(2):
        padded = extend(marine_condition_bundle, 1)
        marine_condition_bundle = substep(padded, row_angles(own_rows, total_rows))
    layer_ordinal_index = thermal_anomaly_field.shape[0]
    return (
        marine_condition_bundle[:layer_ordinal_index],
        marine_condition_bundle[layer_ordinal_index : 2 * layer_ordinal_index],
        marine_condition_bundle[2 * layer_ordinal_index : 3 * layer_ordinal_index],
        marine_condition_bundle[3 * layer_ordinal_index : 4 * layer_ordinal_index],
    )


def solution(mesh):
    placed = (
        P(None, "lat", "lon"),
        P(None, "lat", "lon"),
        P(None, "lat", "lon"),
        P(None, "lat", "lon"),
        P("lat", "lon"),
        P("lat", "lon"),
    )
    return jax.shard_map(
        on_device,
        mesh=mesh,
        in_specs=placed,
        out_specs=(
            P(None, "lat", "lon"),
            P(None, "lat", "lon"),
            P(None, "lat", "lon"),
            P(None, "lat", "lon"),
        ),
        check_vma=False,
    )
```

profile of v0, /device:TPU:6, one launch (start us, length us, event | category | flops | bytes accessed | tf_op | source)
XLA Modules:
  0.0 174.0 jit_solution(11072964726335190651)
XLA Ops:
  0.7 1.0 constant_dynamic-update-slice_fusion.4
  1.7 1.0 constant_dynamic-update-slice_fusion.3
  3.9 17.6 %collective-permute-start.1 = (f32[65,32,1]{0,1,2:T(8,128)S(1)}, f32[65,32,1]{0,1,2:T(8,128)S(1)}, u32[]{:S(2)}, u32[]{:S(2)}) collective-permute-start(f32[65,32,1]{0,1,2:T(8,128)S(1)} %copy.52), channel_id=1, source_target_pairs={{1,0},{2,1},{3,2},{4,3},{5,4},{6,5},{7,6},{8,7},{9,8},{10,9},{11,1... | collective-permute-start | bytes 24968 | tf_op jit(solution)/shard_map/ppermute | solution.py:21
  22.2 1.9 %collective-permute-start = (f32[65,32,1]{0,1,2:T(8,128)S(1)}, f32[65,32,1]{0,1,2:T(8,128)S(1)}, u32[]{:S(2)}, u32[]{:S(2)}) collective-permute-start(f32[65,32,1]{0,1,2:T(8,128)S(1)} %copy.51), channel_id=1, source_target_pairs={{0,1},{1,2},{2,3},{3,4},{4,5},{5,6},{6,7},{7,8},{8,9},{9,10},{10,1... | collective-permute-start | bytes 24968 | tf_op jit(solution)/shard_map/ppermute | solution.py:19
  24.1 1.0 copy.54
  25.2 12.9 %collective-permute-done = f32[65,32,1]{0,1,2:T(8,128)S(1)} collective-permute-done((f32[65,32,1]{0,1,2:T(8,128)S(1)}, f32[65,32,1]{0,1,2:T(8,128)S(1)}, u32[]{:S(2)}, u32[]{:S(2)}) %collective-permute-start) | collective-permute-done | bytes 8352 | tf_op jit(solution)/shard_map/ppermute | solution.py:19
  38.1 1.0 copy.53
  39.7 1.9 %collective-permute-start.3 = (f32[65,1,130]{0,2,1:T(8,128)S(1)}, f32[65,1,130]{0,2,1:T(8,128)S(1)}, u32[]{:S(2)}, u32[]{:S(2)}) collective-permute-start(f32[65,1,130]{0,2,1:T(8,128)S(1)} %copy.55), channel_id=1, source_target_pairs={{0,1},{1,0},{2,3},{3,2},{4,5},{5,4},{6,7},{7,6},{8,9},{9,8},{10,11... | collective-permute-start | bytes 101408 | tf_op jit(solution)/shard_map/ppermute | solution.py:29
  41.7 1.2 collective-permute-done.3
  42.9 1.9 %collective-permute-start.4 = (f32[65,1,130]{0,2,1:T(8,128)S(1)}, f32[65,1,130]{0,2,1:T(8,128)}, u32[]{:S(2)}, u32[]{:S(2)}) collective-permute-start(f32[65,1,130]{0,2,1:T(8,128)S(1)} %collective-permute-done.3), channel_id=1, source_target_pairs={{0,2},{1,3},{2,0},{3,1},{4,6},{5,7},{6,4},{7,5},{8,10},{9,11},{10,... | collective-permute-start | bytes 101408 | tf_op jit(solution)/shard_map/ppermute | solution.py:29
  44.8 13.7 %collective-permute-done.4 = f32[65,1,130]{0,2,1:T(8,128)} collective-permute-done((f32[65,1,130]{0,2,1:T(8,128)S(1)}, f32[65,1,130]{0,2,1:T(8,128)}, u32[]{:S(2)}, u32[]{:S(2)}) %collective-permute-start.4) | collective-permute-done | bytes 33832 | tf_op jit(solution)/shard_map/ppermute | solution.py:29
  58.5 1.9 %collective-permute-start.5 = (f32[65,1,130]{0,2,1:T(8,128)}, f32[65,1,130]{0,2,1:T(8,128)}, u32[]{:S(2)}, u32[]{:S(2)}) collective-permute-start(f32[65,1,130]{0,2,1:T(8,128)} %collective-permute-done.4), channel_id=1, source_target_pairs={{0,4},{1,5},{2,6},{3,7},{4,0},{5,1},{6,2},{7,3},{8,12},{9,13},{10,... | collective-permute-start | bytes 101408 | tf_op jit(solution)/shard_map/ppermute | solution.py:29
  60.5 6.7 %collective-permute-start.2 = (f32[65,1,130]{0,2,1:T(8,128)S(1)}, f32[65,1,130]{0,2,1:T(8,128)S(1)}, u32[]{:S(2)}, u32[]{:S(2)}) collective-permute-start(f32[65,1,130]{0,2,1:T(8,128)S(1)} %copy.55), channel_id=1, source_target_pairs={{0,16},{16,32},{32,48},{48,64},{64,80},{80,96},{96,112},{112,128},... | collective-permute-start | bytes 101408 | tf_op jit(solution)/shard_map/ppermute | solution.py:19
  67.3 6.6 %collective-permute-start.7 = (f32[65,1,130]{0,2,1:T(8,128)S(1)}, f32[65,1,130]{0,2,1:T(8,128)}, u32[]{:S(2)}, u32[]{:S(2)}) collective-permute-start(f32[65,1,130]{0,2,1:T(8,128)S(1)} %copy.58), channel_id=1, source_target_pairs={{16,0},{32,16},{48,32},{64,48},{80,64},{96,80},{112,96},{128,112},... | collective-permute-start | bytes 101408 | tf_op jit(solution)/shard_map/ppermute | solution.py:21
  73.9 2.8 %collective-permute-start.6 = (f32[65,1,130]{0,2,1:T(8,128)}, f32[65,1,130]{0,2,1:T(8,128)}, u32[]{:S(2)}, u32[]{:S(2)}) collective-permute-start(f32[65,1,130]{0,2,1:T(8,128)} %collective-permute-done.5), channel_id=1, source_target_pairs={{0,8},{1,9},{2,10},{3,11},{4,12},{5,13},{6,14},{7,15},{8,0},{9,1},... | collective-permute-start | bytes 101408 | tf_op jit(solution)/shard_map/ppermute | solution.py:29
  76.8 1.0 copy.59
  77.9 4.1 %collective-permute-done.6 = f32[65,1,130]{0,2,1:T(8,128)} collective-permute-done((f32[65,1,130]{0,2,1:T(8,128)}, f32[65,1,130]{0,2,1:T(8,128)}, u32[]{:S(2)}, u32[]{:S(2)}) %collective-permute-start.6) | collective-permute-done | bytes 33832 | tf_op jit(solution)/shard_map/ppermute | solution.py:29
  82.0 1.0 copy.57
  84.1 0.8 copy-done.2
  88.6 0.9 constant_dynamic-update-slice_fusion.9
  89.7 1.0 copy-done.1
  90.8 2.0 %constant_dynamic-update-slice_fusion.7 = (f32[65,32,128]{2,1,0:T(8,128)S(1)}, f32[16,32,128]{2,1,0:T(8,128)}, f32[16,32,128]{2,1,0:T(8,128)S(1)}, f32[16,32,128]{2,1,0:T(8,128)S(1)}) fusion(f32[65,32,128]{2,1,0:T(8,128)S(1)} %get-tuple-element.21, f32[32]{0:T(128)S(1)} %get-tuple-element.45, f32[32]{0:T(128)S(1)} %get-tuple-element.46, ...), kind=kLoop, calls=%fused_computation.265 | loop fusion | flops 3538944 | bytes 8309760
  92.9 0.9 constant_dynamic-update-slice_fusion.6
  94.9 2.1 %collective-permute-start.9 = (f32[65,32,1]{0,1,2:T(8,128)S(1)}, f32[65,32,1]{0,1,2:T(8,128)S(1)}, u32[]{:S(2)}, u32[]{:S(2)}) collective-permute-start(f32[65,32,1]{0,1,2:T(8,128)S(1)} %copy.65), channel_id=1, source_target_pairs={{1,0},{2,1},{3,2},{4,3},{5,4},{6,5},{7,6},{8,7},{9,8},{10,9},{11,1... | collective-permute-start | bytes 24968 | tf_op jit(solution)/shard_map/ppermute | solution.py:21
  97.7 2.4 %collective-permute-start.8 = (f32[65,32,1]{0,1,2:T(8,128)S(1)}, f32[65,32,1]{0,1,2:T(8,128)S(1)}, u32[]{:S(2)}, u32[]{:S(2)}) collective-permute-start(f32[65,32,1]{0,1,2:T(8,128)S(1)} %copy.64), channel_id=1, source_target_pairs={{0,1},{1,2},{2,3},{3,4},{4,5},{5,6},{6,7},{7,8},{8,9},{9,10},{10,1... | collective-permute-start | bytes 24968 | tf_op jit(solution)/shard_map/ppermute | solution.py:19
  100.1 1.0 copy.67
  101.2 12.4 %collective-permute-done.8 = f32[65,32,1]{0,1,2:T(8,128)S(1)} collective-permute-done((f32[65,32,1]{0,1,2:T(8,128)S(1)}, f32[65,32,1]{0,1,2:T(8,128)S(1)}, u32[]{:S(2)}, u32[]{:S(2)}) %collective-permute-start.8) | collective-permute-done | bytes 8352 | tf_op jit(solution)/shard_map/ppermute | solution.py:19
  113.6 1.0 copy.66
  114.6 1.1 pad_maximum_fusion.22
  115.7 1.6 copy.68
  117.3 1.9 %collective-permute-start.11 = (f32[65,1,130]{0,2,1:T(8,128)}, f32[65,1,130]{0,2,1:T(8,128)S(1)}, u32[]{:S(2)}, u32[]{:S(2)}) collective-permute-start(f32[65,1,130]{0,2,1:T(8,128)} %copy.68), channel_id=1, source_target_pairs={{0,1},{1,0},{2,3},{3,2},{4,5},{5,4},{6,7},{7,6},{8,9},{9,8},{10,11... | collective-permute-start | bytes 101408 | tf_op jit(solution)/shard_map/ppermute | solution.py:29
  119.3 1.4 collective-permute-done.11
  120.7 6.9 %collective-permute-start.12 = (f32[65,1,130]{0,2,1:T(8,128)S(1)}, f32[65,1,130]{0,2,1:T(8,128)}, u32[]{:S(2)}, u32[]{:S(2)}) collective-permute-start(f32[65,1,130]{0,2,1:T(8,128)S(1)} %collective-permute-done.11), channel_id=1, source_target_pairs={{0,2},{1,3},{2,0},{3,1},{4,6},{5,7},{6,4},{7,5},{8,10},{9,11},{10,... | collective-permute-start | bytes 101408 | tf_op jit(solution)/shard_map/ppermute | solution.py:29
  127.6 8.1 %collective-permute-done.12 = f32[65,1,130]{0,2,1:T(8,128)} collective-permute-done((f32[65,1,130]{0,2,1:T(8,128)S(1)}, f32[65,1,130]{0,2,1:T(8,128)}, u32[]{:S(2)}, u32[]{:S(2)}) %collective-permute-start.12) | collective-permute-done | bytes 33832 | tf_op jit(solution)/shard_map/ppermute | solution.py:29
  135.7 2.7 %collective-permute-start.13 = (f32[65,1,130]{0,2,1:T(8,128)}, f32[65,1,130]{0,2,1:T(8,128)}, u32[]{:S(2)}, u32[]{:S(2)}) collective-permute-start(f32[65,1,130]{0,2,1:T(8,128)} %collective-permute-done.12), channel_id=1, source_target_pairs={{0,4},{1,5},{2,6},{3,7},{4,0},{5,1},{6,2},{7,3},{8,12},{9,13},{10,... | collective-permute-start | bytes 101408 | tf_op jit(solution)/shard_map/ppermute | solution.py:29
  138.4 0.7 copy.71
  139.2 6.9 %collective-permute-start.15 = (f32[65,1,130]{0,2,1:T(8,128)}, f32[65,1,130]{0,2,1:T(8,128)S(1)}, u32[]{:S(2)}, u32[]{:S(2)}) collective-permute-start(f32[65,1,130]{0,2,1:T(8,128)} %copy.71), channel_id=1, source_target_pairs={{16,0},{32,16},{48,32},{64,48},{80,64},{96,80},{112,96},{128,112},... | collective-permute-start | bytes 101408 | tf_op jit(solution)/shard_map/ppermute | solution.py:21
  146.0 1.9 %collective-permute-start.10 = (f32[65,1,130]{0,2,1:T(8,128)}, f32[65,1,130]{0,2,1:T(8,128)}, u32[]{:S(2)}, u32[]{:S(2)}) collective-permute-start(f32[65,1,130]{0,2,1:T(8,128)} %copy.68), channel_id=1, source_target_pairs={{0,16},{16,32},{32,48},{48,64},{64,80},{80,96},{96,112},{112,128},... | collective-permute-start | bytes 101408 | tf_op jit(solution)/shard_map/ppermute | solution.py:19
  148.0 1.9 %collective-permute-start.14 = (f32[65,1,130]{0,2,1:T(8,128)}, f32[65,1,130]{0,2,1:T(8,128)}, u32[]{:S(2)}, u32[]{:S(2)}) collective-permute-start(f32[65,1,130]{0,2,1:T(8,128)} %collective-permute-done.13), channel_id=1, source_target_pairs={{0,8},{1,9},{2,10},{3,11},{4,12},{5,13},{6,14},{7,15},{8,0},{9,1},... | collective-permute-start | bytes 101408 | tf_op jit(solution)/shard_map/ppermute | solution.py:29
  149.9 0.7 copy.72
  150.6 9.4 %collective-permute-done.10 = f32[65,1,130]{0,2,1:T(8,128)} collective-permute-done((f32[65,1,130]{0,2,1:T(8,128)}, f32[65,1,130]{0,2,1:T(8,128)}, u32[]{:S(2)}, u32[]{:S(2)}) %collective-permute-start.10) | collective-permute-done | bytes 33832 | tf_op jit(solution)/shard_map/ppermute | solution.py:19
  160.1 1.0 copy.73
  161.0 1.6 copy.70
  162.6 1.9 %reverse.1 = f32[65,1,256]{2,1,0:T(1,128)} reverse(f32[65,1,256]{2,1,0:T(1,128)} %bitcast.13), dimensions={1,2} | reverse | bytes 133120
  164.6 1.2 broadcast_select_fusion
  169.9 0.9 fusion.95
  170.9 2.0 %subtract_multiply_fusion = (f32[16,32,128]{2,1,0:T(8,128)}, f32[16,32,128]{2,1,0:T(8,128)S(1)}, f32[16,32,128]{2,1,0:T(8,128)S(1)}) fusion(f32[16,34,130]{2,1,0:T(8,128)S(1)} %fusion, f32[32]{0:T(128)S(1)} %get-tuple-element.45, f32[32]{0:T(128)S(1)} %get-tuple-element.46, f32[16,32,128]{2,1,0:T(8,128)S(1)} %copy-done.5, f32[65,32,1]{2,1,0:T(8,128)S(1)} %copy.67, ...), kind=kLoop, calls=%fused_computation.226 | loop fusion | flops 3538944 | bytes 5868048 | tf_op jit(solution)/shard_map/mul | solution.py:95
  173.0 1.1 add_multiply_fusion
  (69 shorter events, 13.9 us)
Async XLA Ops:
  0.6 2.0 %copy-start.6 = (f32[16,32,128]{2,1,0:T(8,128)S(1)}, f32[16,32,128]{2,1,0:T(8,128)}, u32[]{:S(2)}) copy-start(f32[16,32,128]{2,1,0:T(8,128)} %param.8) | copy-start | bytes 786436
  0.6 2.1 %copy-start.8 = (f32[16,32,128]{2,1,0:T(8,128)S(1)}, f32[16,32,128]{2,1,0:T(8,128)}, u32[]{:S(2)}) copy-start(f32[16,32,128]{2,1,0:T(8,128)} %param.9) | copy-start | bytes 786436
  0.7 2.1 %copy-start.11 = (s32[32,128]{1,0:T(8,128)S(1)}, s32[32,128]{1,0:T(8,128)}, u32[]{:S(2)}) copy-start(s32[32,128]{1,0:T(8,128)} %param.10) | copy-start | bytes 49156
  0.7 2.1 %copy-start.12 = (s32[32,128]{1,0:T(8,128)S(1)}, s32[32,128]{1,0:T(8,128)}, u32[]{:S(2)}) copy-start(s32[32,128]{1,0:T(8,128)} %param.11) | copy-start | bytes 49156
  3.9 20.2 %collective-permute-start.1 = (f32[65,32,1]{0,1,2:T(8,128)S(1)}, f32[65,32,1]{0,1,2:T(8,128)S(1)}, u32[]{:S(2)}, u32[]{:S(2)}) collective-permute-start(f32[65,32,1]{0,1,2:T(8,128)S(1)} %copy.52), channel_id=1, source_target_pairs={{1,0},{2,1},{3,2},{4,3},{5,4},{6,5},{7,6},{8,7},{9,8},{10,9},{11,1... | collective-permute-start | bytes 24968 | tf_op jit(solution)/shard_map/ppermute | solution.py:21
  22.2 15.9 %collective-permute-start = (f32[65,32,1]{0,1,2:T(8,128)S(1)}, f32[65,32,1]{0,1,2:T(8,128)S(1)}, u32[]{:S(2)}, u32[]{:S(2)}) collective-permute-start(f32[65,32,1]{0,1,2:T(8,128)S(1)} %copy.51), channel_id=1, source_target_pairs={{0,1},{1,2},{2,3},{3,4},{4,5},{5,6},{6,7},{7,8},{8,9},{9,10},{10,1... | collective-permute-start | bytes 24968 | tf_op jit(solution)/shard_map/ppermute | solution.py:19
  39.1 48.9 %copy-start = (f32[65,32,1]{2,1,0:T(8,128)}, f32[65,32,1]{2,1,0:T(8,128)S(1)}, u32[]{:S(2)}) copy-start(f32[65,32,1]{2,1,0:T(8,128)S(1)} %copy.53) | copy-start | bytes 24964
  39.7 3.2 %collective-permute-start.3 = (f32[65,1,130]{0,2,1:T(8,128)S(1)}, f32[65,1,130]{0,2,1:T(8,128)S(1)}, u32[]{:S(2)}, u32[]{:S(2)}) collective-permute-start(f32[65,1,130]{0,2,1:T(8,128)S(1)} %copy.55), channel_id=1, source_target_pairs={{0,1},{1,0},{2,3},{3,2},{4,5},{5,4},{6,7},{7,6},{8,9},{9,8},{10,11... | collective-permute-start | bytes 101408 | tf_op jit(solution)/shard_map/ppermute | solution.py:29
  42.9 15.6 %collective-permute-start.4 = (f32[65,1,130]{0,2,1:T(8,128)S(1)}, f32[65,1,130]{0,2,1:T(8,128)}, u32[]{:S(2)}, u32[]{:S(2)}) collective-permute-start(f32[65,1,130]{0,2,1:T(8,128)S(1)} %collective-permute-done.3), channel_id=1, source_target_pairs={{0,2},{1,3},{2,0},{3,1},{4,6},{5,7},{6,4},{7,5},{8,10},{9,11},{10,... | collective-permute-start | bytes 101408 | tf_op jit(solution)/shard_map/ppermute | solution.py:29
  58.5 15.4 %collective-permute-start.5 = (f32[65,1,130]{0,2,1:T(8,128)}, f32[65,1,130]{0,2,1:T(8,128)}, u32[]{:S(2)}, u32[]{:S(2)}) collective-permute-start(f32[65,1,130]{0,2,1:T(8,128)} %collective-permute-done.4), channel_id=1, source_target_pairs={{0,4},{1,5},{2,6},{3,7},{4,0},{5,1},{6,2},{7,3},{8,12},{9,13},{10,... | collective-permute-start | bytes 101408 | tf_op jit(solution)/shard_map/ppermute | solution.py:29
  60.5 17.3 %collective-permute-start.2 = (f32[65,1,130]{0,2,1:T(8,128)S(1)}, f32[65,1,130]{0,2,1:T(8,128)S(1)}, u32[]{:S(2)}, u32[]{:S(2)}) collective-permute-start(f32[65,1,130]{0,2,1:T(8,128)S(1)} %copy.55), channel_id=1, source_target_pairs={{0,16},{16,32},{32,48},{48,64},{64,80},{80,96},{96,112},{112,128},... | collective-permute-start | bytes 101408 | tf_op jit(solution)/shard_map/ppermute | solution.py:19
  67.3 9.5 %collective-permute-start.7 = (f32[65,1,130]{0,2,1:T(8,128)S(1)}, f32[65,1,130]{0,2,1:T(8,128)}, u32[]{:S(2)}, u32[]{:S(2)}) collective-permute-start(f32[65,1,130]{0,2,1:T(8,128)S(1)} %copy.58), channel_id=1, source_target_pairs={{16,0},{32,16},{48,32},{64,48},{80,64},{96,80},{112,96},{128,112},... | collective-permute-start | bytes 101408 | tf_op jit(solution)/shard_map/ppermute | solution.py:21
  73.9 8.0 %collective-permute-start.6 = (f32[65,1,130]{0,2,1:T(8,128)}, f32[65,1,130]{0,2,1:T(8,128)}, u32[]{:S(2)}, u32[]{:S(2)}) collective-permute-start(f32[65,1,130]{0,2,1:T(8,128)} %collective-permute-done.5), channel_id=1, source_target_pairs={{0,8},{1,9},{2,10},{3,11},{4,12},{5,13},{6,14},{7,15},{8,0},{9,1},... | collective-permute-start | bytes 101408 | tf_op jit(solution)/shard_map/ppermute | solution.py:29
  83.9 1.0 copy-start.2
  83.9 1.0 copy-start.3
  89.5 1.2 copy-start.1
  89.5 1.3 copy-start.7
  89.5 1.3 copy-start.9
  94.9 5.2 %collective-permute-start.9 = (f32[65,32,1]{0,1,2:T(8,128)S(1)}, f32[65,32,1]{0,1,2:T(8,128)S(1)}, u32[]{:S(2)}, u32[]{:S(2)}) collective-permute-start(f32[65,32,1]{0,1,2:T(8,128)S(1)} %copy.65), channel_id=1, source_target_pairs={{1,0},{2,1},{3,2},{4,3},{5,4},{6,5},{7,6},{8,7},{9,8},{10,9},{11,1... | collective-permute-start | bytes 24968 | tf_op jit(solution)/shard_map/ppermute | solution.py:21
  97.7 15.9 %collective-permute-start.8 = (f32[65,32,1]{0,1,2:T(8,128)S(1)}, f32[65,32,1]{0,1,2:T(8,128)S(1)}, u32[]{:S(2)}, u32[]{:S(2)}) collective-permute-start(f32[65,32,1]{0,1,2:T(8,128)S(1)} %copy.64), channel_id=1, source_target_pairs={{0,1},{1,2},{2,3},{3,4},{4,5},{5,6},{6,7},{7,8},{8,9},{9,10},{10,1... | collective-permute-start | bytes 24968 | tf_op jit(solution)/shard_map/ppermute | solution.py:19
  117.3 3.4 %collective-permute-start.11 = (f32[65,1,130]{0,2,1:T(8,128)}, f32[65,1,130]{0,2,1:T(8,128)S(1)}, u32[]{:S(2)}, u32[]{:S(2)}) collective-permute-start(f32[65,1,130]{0,2,1:T(8,128)} %copy.68), channel_id=1, source_target_pairs={{0,1},{1,0},{2,3},{3,2},{4,5},{5,4},{6,7},{7,6},{8,9},{9,8},{10,11... | collective-permute-start | bytes 101408 | tf_op jit(solution)/shard_map/ppermute | solution.py:29
  120.7 15.0 %collective-permute-start.12 = (f32[65,1,130]{0,2,1:T(8,128)S(1)}, f32[65,1,130]{0,2,1:T(8,128)}, u32[]{:S(2)}, u32[]{:S(2)}) collective-permute-start(f32[65,1,130]{0,2,1:T(8,128)S(1)} %collective-permute-done.11), channel_id=1, source_target_pairs={{0,2},{1,3},{2,0},{3,1},{4,6},{5,7},{6,4},{7,5},{8,10},{9,11},{10,... | collective-permute-start | bytes 101408 | tf_op jit(solution)/shard_map/ppermute | solution.py:29
  135.7 12.3 %collective-permute-start.13 = (f32[65,1,130]{0,2,1:T(8,128)}, f32[65,1,130]{0,2,1:T(8,128)}, u32[]{:S(2)}, u32[]{:S(2)}) collective-permute-start(f32[65,1,130]{0,2,1:T(8,128)} %collective-permute-done.12), channel_id=1, source_target_pairs={{0,4},{1,5},{2,6},{3,7},{4,0},{5,1},{6,2},{7,3},{8,12},{9,13},{10,... | collective-permute-start | bytes 101408 | tf_op jit(solution)/shard_map/ppermute | solution.py:29
  139.2 10.7 %collective-permute-start.15 = (f32[65,1,130]{0,2,1:T(8,128)}, f32[65,1,130]{0,2,1:T(8,128)S(1)}, u32[]{:S(2)}, u32[]{:S(2)}) collective-permute-start(f32[65,1,130]{0,2,1:T(8,128)} %copy.71), channel_id=1, source_target_pairs={{16,0},{32,16},{48,32},{64,48},{80,64},{96,80},{112,96},{128,112},... | collective-permute-start | bytes 101408 | tf_op jit(solution)/shard_map/ppermute | solution.py:21
  146.0 14.0 %collective-permute-start.10 = (f32[65,1,130]{0,2,1:T(8,128)}, f32[65,1,130]{0,2,1:T(8,128)}, u32[]{:S(2)}, u32[]{:S(2)}) collective-permute-start(f32[65,1,130]{0,2,1:T(8,128)} %copy.68), channel_id=1, source_target_pairs={{0,16},{16,32},{32,48},{48,64},{64,80},{80,96},{96,112},{112,128},... | collective-permute-start | bytes 101408 | tf_op jit(solution)/shard_map/ppermute | solution.py:19
  148.0 13.1 %collective-permute-start.14 = (f32[65,1,130]{0,2,1:T(8,128)}, f32[65,1,130]{0,2,1:T(8,128)}, u32[]{:S(2)}, u32[]{:S(2)}) collective-permute-start(f32[65,1,130]{0,2,1:T(8,128)} %collective-permute-done.13), channel_id=1, source_target_pairs={{0,8},{1,9},{2,10},{3,11},{4,12},{5,13},{6,14},{7,15},{8,0},{9,1},... | collective-permute-start | bytes 101408 | tf_op jit(solution)/shard_map/ppermute | solution.py:29
  168.8 1.0 copy-start.4
  169.9 1.0 copy-start.5
  169.9 1.0 copy-start.10
where the time goes:
time: 175 us; the launch traced here: 174 us
  starting transfers between devices  68.1 us (39%)
  waiting for transfers between devices  63.3 us (36%)
  local copies, waits for them, and re-layouts  22.9 us (13%)
  other arithmetic  18.6 us (11%)
    ppermute x4, waiting for transfers between devices, with_halo(): lax.ppermute(tail, axis, [(i, (i + 1) % count) for i in range(ends)])  34.7 us
    ppermute x4, starting transfers between devices, with_halo(): lax.ppermute(head, axis, [((i + 1) % count, i) for i in range(ends)])  33.2 us
    ppermute x8, waiting for transfers between devices, swapped(): lax.ppermute(array, axis, [(i, i ^ 1 << stride) for i in range(lax.axis_s...  28.5 us
    ppermute x8, starting transfers between devices, swapped(): lax.ppermute(array, axis, [(i, i ^ 1 << stride) for i in range(lax.axis_s...  22 us
    ppermute x4, starting transfers between devices, with_halo(): lax.ppermute(tail, axis, [(i, (i + 1) % count) for i in range(ends)])  13 us
    unnamed x32, local copies, waits for them, and re-layouts  7.11 us
    add x8, other arithmetic, transport(): jnp.maximum(north_face, 0.0) * quantity[:, :-1, 1:-1]  4.69 us
    unnamed x4, other arithmetic  4.04 us
  transfers between devices with their start and end apart: 16, of which 8 were waited for; matrix products, arithmetic and copies ran while one was open for 4% of the time, Pallas kernels for 0%

commit v1 on v0

v1 whole, which is shorter than its diff:
```python
import jax
import jax.numpy as jnp
from jax import lax
from jax.experimental import pallas as pl
from jax.experimental.pallas import tpu as pltpu
from jax.sharding import PartitionSpec as P

MIXING = 0.2
VISCOSITY = 0.05
ROTATION = 0.3
LEVELS = 16
ROWS = 32
LANES = 128
N_LAT = 32
N_LON = 16
BLOCK = 8
ROW_MSG = 136
COL_MSG = 48
EDGE_MSG = COL_MSG + ROW_MSG + 8


def near_lon(lat, lon):
    return lat, lon ^ 1


def far_lon(lat, lon):
    return lat, (lon + 1) % N_LON if lon % 2 else (lon - 1) % N_LON


def even_lat(lat, lon):
    return lat ^ 1, lon


def odd_lat(lat, lon):
    if lat == N_LAT - 1:
        return lat, N_LON - 1 - lon
    return (lat + 1 if lat % 2 else lat - 1), lon


def is_edge(lat):
    return lat > 0 and lat % BLOCK in (0, BLOCK - 1)


def pairs(where_to, member):
    found = []
    for lat in range(N_LAT):
        for lon in range(N_LON):
            if member(lat):
                to_lat, to_lon = where_to(lat, lon)
                found.append((lat * N_LON + lon, to_lat * N_LON + to_lon))
    return found


def send(array, where_to, member):
    return lax.ppermute(array, ("lat", "lon"), pairs(where_to, member))


def odd_or_diagonal(lat, lon):
    to = odd_lat(lat, lon)
    return far_lon(*to) if is_edge(lat) else to


def near_corner_relay(lat, lon):
    return far_lon(*near_lon(*odd_lat(lat, lon)))


def shift(x, by, axis=1):
    by = by % x.shape[axis]
    return x if by == 0 else pltpu.roll(x, by, axis)


def lanes_of(shape):
    return lax.broadcasted_iota(jnp.int32, shape, 1)


def position():
    return lax.axis_index("lat"), lax.axis_index("lon")


def pack_kernel(heat, salt, zonal, merid, flag, tally, row_even, row_odd, packed, col_near, col_far):
    lat, lon = position()
    lat_odd = lax.rem(lat, 2) == 1
    lon_odd = lax.rem(lon, 2) == 1
    depth = (flag[...] * tally[...]).astype(jnp.float32)
    lane = lanes_of((ROWS, LANES))
    group = lane >> 3
    pair = (lane & 7) >> 1
    west = jnp.zeros((ROWS, LANES), jnp.float32)
    east = west
    for f, field in enumerate((heat, salt, zonal, merid)):
        acc = jnp.zeros((ROWS, LANES), jnp.float32)
        for k in range(LEVELS):
            acc = jnp.where(group == k, shift(field[k], 8 * k + 2), acc)
        packed[f] = acc
        west = jnp.where(pair == f, shift(acc, 2 * f - 2), west)
        east = jnp.where(pair == f, shift(acc, 2 * f), east)
        for d in range(2):
            at = (d * 4 + f) * LEVELS
            top = field[:, ROWS - 1 - d, :]
            bottom = field[:, d, :]
            row_even[at : at + LEVELS, :] = jnp.where(lat_odd, bottom, top)
            row_odd[at : at + LEVELS, :] = jnp.where(lat_odd, top, bottom)
    short = lanes_of((8, LANES)) >> 1
    depth_west = jnp.zeros((8, LANES), jnp.float32)
    depth_east = depth_west
    for i in range(4):
        part = depth[8 * i : 8 * i + 8]
        depth_west = jnp.where(short == i, shift(part, 2 * i), depth_west)
        depth_east = jnp.where(short == i, shift(part, 2 * i + 2), depth_east)
    col_near[0:ROWS, :] = jnp.where(lon_odd, west, east)
    col_far[0:ROWS, :] = jnp.where(lon_odd, east, west)
    col_near[ROWS : ROWS + 8, :] = jnp.where(lon_odd, depth_west, depth_east)
    col_far[ROWS : ROWS + 8, :] = jnp.where(lon_odd, depth_east, depth_west)
    blank = jnp.zeros((4, LANES), jnp.float32)
    tops = jnp.concatenate([depth[31:32], depth[30:31], west[31:32], east[31:32], blank], 0)
    bottoms = jnp.concatenate([depth[0:1], depth[1:2], west[0:1], east[0:1], blank], 0)
    row_even[128:136, :] = jnp.where(lat_odd, bottoms, tops)
    row_odd[128:136, :] = jnp.where(lat_odd, tops, bottoms)


def relay_kernel(even, odd, near_corner, col_near, col_far, to_near, to_far, to_far_edge):
    _, lon = position()
    lon_odd = lax.rem(lon, 2) == 1
    blank = jnp.zeros((4, LANES), jnp.float32)
    info_even = even[128:136, :]
    info_odd = odd[128:136, :]

    def corners(row):
        return jnp.concatenate(
            [info_even[row : row + 1], info_odd[row : row + 1], info_even[0:1], info_odd[0:1], blank], 0
        )

    west, east = corners(2), corners(3)
    to_near[0:40, :] = col_near[...]
    to_near[40:48, :] = jnp.where(lon_odd, west, east)
    far_tile = jnp.where(lon_odd, east, west)
    to_far[0:40, :] = col_far[...]
    to_far[40:48, :] = far_tile
    to_far_edge[0:40, :] = col_far[...]
    to_far_edge[40:48, :] = far_tile
    to_far_edge[48:184, :] = odd[...]
    to_far_edge[184:192, :] = near_corner[...]


def reversed_lanes(x):
    lane = lanes_of(x.shape)
    for b in range(7):
        x = jnp.where((lane >> b) & 1 == 1, shift(x, 1 << b), shift(x, -(1 << b)))
    return x


def five_point(c, e, w, n, s, up, down, wet, wets, wet_up, wet_down, cosine, sine):
    wet_e, wet_w, wet_n, wet_s = (wet * x for x in wets)
    flow_e = 0.5 * (c[2] + e[2]) * wet_e
    flow_w = 0.5 * (c[2] + w[2]) * wet_w
    flow_n = 0.5 * (c[3] + n[3]) * wet_n
    flow_s = 0.5 * (c[3] + s[3]) * wet_s

    def gain(f, viscosity):
        east = (jnp.maximum(flow_e, 0.0) * c[f] + jnp.minimum(flow_e, 0.0) * e[f]) - viscosity * wet_e * (e[f] - c[f])
        west = (jnp.maximum(flow_w, 0.0) * w[f] + jnp.minimum(flow_w, 0.0) * c[f]) - viscosity * wet_w * (c[f] - w[f])
        north = (jnp.maximum(flow_n, 0.0) * c[f] + jnp.minimum(flow_n, 0.0) * n[f]) - viscosity * wet_n * (n[f] - c[f])
        south = (jnp.maximum(flow_s, 0.0) * s[f] + jnp.minimum(flow_s, 0.0) * c[f]) - viscosity * wet_s * (c[f] - s[f])
        return c[f] - ((east - west) + (north - south))

    def tracer(f):
        mixed = MIXING * ((up[f] - c[f]) * (wet * wet_up) - (c[f] - down[f]) * (wet * wet_down))
        return wet * (gain(f, 0.0) + mixed)

    ua, va = gain(2, VISCOSITY), gain(3, VISCOSITY)
    return [tracer(0), tracer(1), wet * (cosine * ua + sine * va), wet * (cosine * va - sine * ua)]


def north_of(x, last):
    return jnp.concatenate([x[1:], last], 0)


def south_of(x, first):
    return jnp.concatenate([first, x[:-1]], 0)


def as_wet(mask):
    return jnp.where(mask, 1.0, 0.0)


def step_kernel(
    heat, salt, zonal, merid, flag, tally, packed, angles, even, odd, near, far, far_edge,
    heat_out, salt_out, zonal_out, merid_out, mid,
):
    lat, lon = position()
    lat_odd = lax.rem(lat, 2) == 1
    lon_odd = lax.rem(lon, 2) == 1
    at_top = lat == N_LAT - 1
    run = lax.rem(lat, BLOCK)
    edge = jnp.logical_and(lat > 0, jnp.logical_or(run == 0, run == BLOCK - 1))
    fields = (heat, salt, zonal, merid)
    lane = lanes_of((ROWS, LANES))
    place = lane & 7
    level = (lane >> 3).astype(jnp.float32)
    lane1 = lanes_of((1, LANES))
    place1 = lane1 & 7
    depth = (flag[...] * tally[...]).astype(jnp.float32)
    cosine, sine = angles[0:32, :], angles[32:64, :]

    signs = jnp.where(jnp.logical_and(at_top, place1 >= 4), -1.0, 1.0)

    def swap_pair(x):
        return jnp.where(lane1 & 1 == 1, shift(x, 1), shift(x, -1)) * signs

    def unfold_info(info):
        drow, west, east = info[0:1], info[2:3], info[3:4]
        return (
            jnp.where(at_top, reversed_lanes(drow), drow),
            jnp.where(at_top, swap_pair(east), west),
            jnp.where(at_top, swap_pair(west), east),
        )

    odd_rows = jnp.where(edge, far_edge[48:184, :], odd[...])
    turned = reversed_lanes(odd_rows)
    row_field = (lax.broadcasted_iota(jnp.int32, (ROW_MSG, LANES), 0) >> 4) & 3
    below = lax.broadcasted_iota(jnp.int32, (ROW_MSG, LANES), 0) < 128
    turned = jnp.where(jnp.logical_and(below, row_field >= 2), -turned, turned)
    odd_rows = jnp.where(at_top, turned, odd_rows)
    even_rows = even[...]
    south_rows = jnp.where(lat_odd, even_rows, odd_rows)
    north_rows = jnp.where(lat_odd, odd_rows, even_rows)
    far_cols = jnp.where(edge, far_edge[0:48, :], far[...])
    near_cols = near[...]
    west_cols = jnp.where(lon_odd, near_cols, far_cols)
    east_cols = jnp.where(lon_odd, far_cols, near_cols)

    q_depth, q_west, q_east = unfold_info(odd[128:136, :])
    s_depth, s_west, s_east = unfold_info(far_edge[184:192, :])
    far_corner = jnp.where(lon_odd, q_west, q_east)
    near_corner = jnp.where(lon_odd, s_east, s_west)
    west_odd = jnp.where(edge, jnp.where(lon_odd, near_corner, far_corner), west_cols[41:42])
    east_odd = jnp.where(edge, jnp.where(lon_odd, far_corner, near_corner), east_cols[41:42])
    west_odd_depth = jnp.where(edge, jnp.where(lon_odd, s_depth, q_depth), west_cols[43:44])
    east_odd_depth = jnp.where(edge, jnp.where(lon_odd, q_depth, s_depth), east_cols[43:44])

    def by_side(even_part, odd_part):
        return jnp.where(lat_odd, even_part, odd_part), jnp.where(lat_odd, odd_part, even_part)

    sw, nw = by_side(west_cols[40:41], west_odd)
    se, ne = by_side(east_cols[40:41], east_odd)
    sw_d, nw_d = by_side(west_cols[42:43], west_odd_depth)
    se_d, ne_d = by_side(east_cols[42:43], east_odd_depth)
    corner_depth = [(x[:, 127:128], y[:, 0:1]) for x, y in ((sw_d, se_d), (nw_d, ne_d))]

    cols, cols_s, cols_n = [], [], []
    for f in range(4):
        own = packed[f]
        x = jnp.where(place < 2, own, shift(own, 4))
        x = jnp.where((place >> 1) == 1, shift(east_cols[0:32], 2 - 2 * f), x)
        x = jnp.where((place >> 1) == 2, shift(west_cols[0:32], 4 - 2 * f), x)
        cols.append(x)
        for out, w, e in ((cols_s, sw, se), (cols_n, nw, ne)):
            out.append(
                jnp.where(place1 == 5, shift(w, 4 - 2 * f), jnp.where(place1 == 2, shift(e, 2 - 2 * f), 0.0))
            )
    west_d = jnp.concatenate([shift(west_cols[32:40], 4 - 2 * i) for i in range(4)], 0)
    east_d = jnp.concatenate([shift(east_cols[32:40], 2 - 2 * i) for i in range(4)], 0)
    col_depth = jnp.where(lane < 2, shift(depth, 2), shift(depth, 6))
    col_depth = jnp.where((lane >> 1) == 1, east_d, col_depth)
    col_depth = jnp.where((lane >> 1) == 2, west_d, col_depth)
    col_depth = jnp.where(lane < 8, col_depth, 0.0)
    for b in (8, 16, 32, 64):
        col_depth = col_depth + shift(col_depth, b)
    corner_rows = [
        jnp.where(place1 == 5, w, jnp.where(place1 == 2, e, 0.0)) for w, e in corner_depth
    ]

    wets = [
        as_wet(level < x)
        for x in (
            shift(col_depth, -1),
            shift(col_depth, 1),
            north_of(col_depth, corner_rows[1]),
            south_of(col_depth, corner_rows[0]),
        )
    ]
    cols_mid = five_point(
        cols,
        [shift(x, -1) for x in cols],
        [shift(x, 1) for x in cols],
        [north_of(x, y) for x, y in zip(cols, cols_n)],
        [south_of(x, y) for x, y in zip(cols, cols_s)],
        [shift(x, -8) for x in cols[:2]],
        [shift(x, 8) for x in cols[:2]],
        as_wet(level < col_depth),
        wets,
        as_wet(level + 1.0 < col_depth),
        as_wet(jnp.logical_and(lane >= 8, level - 1.0 < col_depth)),
        cosine,
        sine,
    )

    lane16 = lanes_of((LEVELS, LANES))
    sub16 = lax.broadcasted_iota(jnp.int32, (LEVELS, LANES), 0)
    lev16 = sub16.astype(jnp.float32)

    def halo_row(rows, corner_cols, corner_d, own_row, north, at):
        c = [rows[f * 16 : f * 16 + 16] for f in range(4)]
        beyond = [rows[64 + f * 16 : 64 + f * 16 + 16] for f in range(4)]
        inner = [x[:, own_row, :] for x in fields]
        d0, d1, d_in = rows[128:129], rows[129:130], depth[own_row : own_row + 1]
        d_w = jnp.where(lane1 == 0, corner_d[0], shift(d0, 1))
        d_e = jnp.where(lane1 == 127, corner_d[1], shift(d0, -1))
        e, w = [], []
        for f in range(4):
            spread_out = jnp.broadcast_to(corner_cols[f], (LEVELS, LANES))
            at_w = jnp.sum(jnp.where(lane16 == 8 * sub16 + 5, spread_out, 0.0), axis=1, keepdims=True)
            at_e = jnp.sum(jnp.where(lane16 == 8 * sub16 + 2, spread_out, 0.0), axis=1, keepdims=True)
            w.append(jnp.where(lane16 == 0, at_w, shift(c[f], 1)))
            e.append(jnp.where(lane16 == 127, at_e, shift(c[f], -1)))
        n, s, d_n, d_s = (beyond, inner, d1, d_in) if north else (inner, beyond, d_in, d1)
        return five_point(
            c, e, w, n, s,
            [north_of(x, x[15:16]) for x in c[:2]],
            [south_of(x, x[0:1]) for x in c[:2]],
            as_wet(lev16 < d0),
            [as_wet(lev16 < x) for x in (d_e, d_w, d_n, d_s)],
            as_wet(lev16 + 1.0 < d0),
            as_wet(jnp.logical_and(sub16 >= 1, lev16 - 1.0 < d0)),
            angles[64 + at : 65 + at, :],
            angles[66 + at : 67 + at, :],
        )

    south_mid = halo_row(south_rows, cols_s, corner_depth[0], 0, False, 0)
    north_mid = halo_row(north_rows, cols_n, corner_depth[1], ROWS - 1, True, 1)

    d_e = jnp.where(lane == 127, shift(col_depth, 125), shift(depth, -1))
    d_w = jnp.where(lane == 0, shift(col_depth, 123), shift(depth, 1))
    d_n = north_of(depth, north_rows[128:129])
    d_s = south_of(depth, south_rows[128:129])
    m_e, m_w, m_n, m_s = (jnp.minimum(depth, x) for x in (d_e, d_w, d_n, d_s))
    last_row = lax.broadcasted_iota(jnp.int32, (ROWS, LANES), 0) == ROWS - 1
    first_row = lax.broadcasted_iota(jnp.int32, (ROWS, LANES), 0) == 0

    def whole_step(read, col_values, rows_s, rows_n, write):
        sides = [jnp.where(place == 2, x, shift(x, -2)) for x in col_values]
        now = [read(f, 0) for f in range(4)]
        carried = [None, None]
        for k in range(LEVELS):
            above = [read(f, k + 1) for f in range(4)] if k + 1 < LEVELS else None
            half_e, half_w, half_n, half_s = (jnp.where(k < x, 0.5, 0.0) for x in (m_e, m_w, m_n, m_s))
            e, w, n, s = [], [], [], []
            for f in range(4):
                x = now[f]
                ends = shift(sides[f], 127 - (8 * k + 2))
                e.append(jnp.where(lane == 127, ends, shift(x, -1)))
                w.append(jnp.where(lane == 0, ends, shift(x, 1)))
                n.append(jnp.where(last_row, rows_n[f][k : k + 1], shift(x, -1, 0)))
                s.append(jnp.where(first_row, rows_s[f][k : k + 1], shift(x, 1, 0)))
            flow_e = (now[2] + e[2]) * half_e
            flow_w = (now[2] + w[2]) * half_w
            flow_n = (now[3] + n[3]) * half_n
            flow_s = (now[3] + s[3]) * half_s
            out_e, in_e = jnp.maximum(flow_e, 0.0), jnp.minimum(flow_e, 0.0)
            in_w, out_w = jnp.maximum(flow_w, 0.0), jnp.minimum(flow_w, 0.0)
            out_n, in_n = jnp.maximum(flow_n, 0.0), jnp.minimum(flow_n, 0.0)
            in_s, out_s = jnp.maximum(flow_s, 0.0), jnp.minimum(flow_s, 0.0)
            kept = 1.0 - ((out_e - out_w) + (out_n - out_s))
            wet = k < depth
            new = []
            for f in range(2):
                x = now[f]
                total = (x * kept - (in_e * e[f] - in_w * w[f])) - (in_n * n[f] - in_s * s[f])
                if above is not None:
                    flux = jnp.where(k + 1 < depth, MIXING * (above[f] - x), 0.0)
                    total = total + flux
                if carried[f] is not None:
                    total = total - carried[f]
                if above is not None:
                    carried[f] = flux
                new.append(jnp.where(wet, total, 0.0))
            thick = 2.0 * VISCOSITY
            vis_e, vis_w, vis_n, vis_s = (thick * x for x in (half_e, half_w, half_n, half_s))
            kept = kept - ((vis_e + vis_w) + (vis_n + vis_s))
            in_e, in_w, in_n, in_s = vis_e - in_e, vis_w + in_w, vis_n - in_n, vis_s + in_s
            ua, va = (
                (now[f] * kept + (in_e * e[f] + in_w * w[f])) + (in_n * n[f] + in_s * s[f]) for f in (2, 3)
            )
            new.append(jnp.where(wet, cosine * ua + sine * va, 0.0))
            new.append(jnp.where(wet, cosine * va - sine * ua, 0.0))
            for f in range(4):
                write(f, k, new[f])
            now = above

    def to_mid(f, k, value):
        mid[f, k] = value

    outs = (heat_out, salt_out, zonal_out, merid_out)

    def to_out(f, k, value):
        outs[f][k] = value

    whole_step(
        lambda f, k: fields[f][k],
        cols,
        [south_rows[f * 16 : f * 16 + 16] for f in range(4)],
        [north_rows[f * 16 : f * 16 + 16] for f in range(4)],
        to_mid,
    )
    whole_step(lambda f, k: mid[f, k], cols_mid, south_mid, north_mid, to_out)


def shapes(*dims):
    return [jax.ShapeDtypeStruct(d, jnp.float32) for d in dims]


def call(kernel, outputs, *operands, scratch=()):
    vmem = pl.BlockSpec(memory_space=pltpu.VMEM)
    return pl.pallas_call(
        kernel,
        out_shape=shapes(*outputs),
        in_specs=[vmem] * len(operands),
        out_specs=[vmem] * len(outputs),
        scratch_shapes=list(scratch),
        compiler_params=pltpu.CompilerParams(vmem_limit_bytes=32 * 1024 * 1024),
    )(*operands)


def angle_table():
    first = lax.axis_index("lat") * ROWS
    total = ROWS * N_LAT
    ids = jnp.concatenate([jnp.arange(ROWS), jnp.array([-1, ROWS])]) + first
    ids = jnp.where(ids >= total, 2 * total - 1 - ids, ids)
    angle = ROTATION * (2.0 * (ids.astype(jnp.float32) + 0.5) / total - 1.0)
    c, s = jnp.cos(angle), jnp.sin(angle)
    column = jnp.concatenate([c[:ROWS], s[:ROWS], c[ROWS:], s[ROWS:], jnp.zeros((4,), jnp.float32)])
    return jnp.broadcast_to(column[:, None], (72, LANES))


def on_device(heat, salt, zonal, merid, flag, tally):
    whole = (heat, salt, zonal, merid, flag, tally)
    row_even, row_odd, packed, col_near, col_far = call(
        pack_kernel,
        [(ROW_MSG, LANES), (ROW_MSG, LANES), (4, ROWS, LANES), (40, LANES), (40, LANES)],
        *whole,
    )
    everyone, edges = (lambda lat: True), is_edge
    corner = send(row_odd[128:136], near_corner_relay, edges)
    odd = send(row_odd, odd_or_diagonal, lambda lat: lat > 0)
    even = send(row_even, even_lat, everyone)
    to_near, to_far, to_far_edge = call(
        relay_kernel,
        [(COL_MSG, LANES), (COL_MSG, LANES), (EDGE_MSG, LANES)],
        even, odd, corner, col_near, col_far,
    )
    far_edge = send(to_far_edge, far_lon, edges)
    far = send(to_far, far_lon, lambda lat: not is_edge(lat))
    near = send(to_near, near_lon, everyone)
    size = (LEVELS, ROWS, LANES)
    return tuple(
        call(
            step_kernel,
            [size] * 4,
            *whole, packed, angle_table(), even, odd, near, far, far_edge,
            scratch=[pltpu.VMEM((4,) + size, jnp.float32)],
        )
    )


def solution(mesh):
    field, column = P(None, "lat", "lon"), P("lat", "lon")
    return jax.shard_map(
        on_device,
        mesh=mesh,
        in_specs=(field,) * 4 + (column,) * 2,
        out_specs=(field,) * 4,
        check_vma=False,
    )
```

time: 175 us -> 57 us (0.33)
  waiting for transfers between devices: 63.3 us -> 18.4 us
  starting transfers between devices: 68.1 us -> 26.7 us
  other arithmetic: 18.6 us -> 0.05 us
  local copies, waits for them, and re-layouts: 22.9 us -> 5.6 us
  Pallas kernels: 0 us -> 5.08 us
    ppermute x16 -> x6, waiting for transfers between devices: 63.3 us -> 18.4 us  [send(): return lax.ppermute(array, ('lat', 'lon'), pairs(where_to, member))]
    ppermute x16 -> x6, starting transfers between devices: 68.1 us -> 26.7 us  [send(): return lax.ppermute(array, ('lat', 'lon'), pairs(where_to, member))]
    ppermute x10 -> x0, local copies, waits for them, and re-layouts: 9.55 us -> none  [the longest x4 3.8 us: with_halo(): lax.ppermute(head, axis, [((i + 1) % count, i) for i in range(ends)])]
    add x12 -> x0, other arithmetic: 6.78 us -> none  [the longest x8 4.69 us: transport(): jnp.maximum(north_face, 0.0) * quantity[:, :-1, 1:-1]]
    slice x10 -> x3, local copies, waits for them, and re-layouts: 6.13 us -> 0.15 us  [the longest x1 0.07 us: angle_table(): c[ROWS:]]
    pallas_call x0 -> x3, Pallas kernels: none -> 5.08 us  [call(): pl.pallas_call(kernel, out_shape=shapes(*outputs), in_specs=[vmem] * len(...]
    mul x5 -> x0, other arithmetic: 4.4 us -> none  [the longest x1 2.02 us: substep(): merid_n = inside * (cosine * merid_a - sine * zonal_a)]
    unnamed x4 -> x0, other arithmetic: 4.04 us -> none
  transfers between devices with their start and end apart: 16 -> 6, of which waited for: 8 -> 2; matrix products, arithmetic and copies ran while one was open for 4% -> 1% of each run, Pallas kernels for 0% -> 0%
where the time goes in v1:
time: 57 us; the launch traced here: 56.6 us
  starting transfers between devices  26.7 us (47%)
  waiting for transfers between devices  18.4 us (32%)
  local copies, waits for them, and re-layouts  5.6 us (10%)
  Pallas kernels  5.08 us (9%)
  between operations  0.81 us (1%)
    ppermute x6, starting transfers between devices, send(): return lax.ppermute(array, ('lat', 'lon'), pairs(where_to, member))  26.7 us
    ppermute x6, waiting for transfers between devices, send(): return lax.ppermute(array, ('lat', 'lon'), pairs(where_to, member))  18.4 us
    unnamed x26, local copies, waits for them, and re-layouts  5.26 us
    pallas_call x3, Pallas kernels, call(): pl.pallas_call(kernel, out_shape=shapes(*outputs), in_specs=[vmem] * len(...  5.08 us
  transfers between devices with their start and end apart: 6, of which 2 were waited for; matrix products, arithmetic and copies ran while one was open for 1% of the time, Pallas kernels for 0%

profile of v1, /device:TPU:6, one launch (start us, length us, event | category | flops | bytes accessed | tf_op | source)
XLA Modules:
  0.0 56.6 jit_solution(7725342950978948770)
XLA Ops:
  0.6 0.0 copy-start
  0.6 0.9 %copy-done = f32[16,32,128]{2,1,0:T(8,128)S(1)} copy-done((f32[16,32,128]{2,1,0:T(8,128)S(1)}, f32[16,32,128]{2,1,0:T(8,128)}, u32[]{:S(2)}) %copy-start) | copy-done | bytes 262168
  1.6 0.0 copy-start.2
  1.6 0.9 %copy-done.2 = f32[16,32,128]{2,1,0:T(8,128)S(1)} copy-done((f32[16,32,128]{2,1,0:T(8,128)S(1)}, f32[16,32,128]{2,1,0:T(8,128)}, u32[]{:S(2)}) %copy-start.2) | copy-done | bytes 262168
  2.5 0.0 copy-start.4
  2.5 0.9 %copy-done.4 = f32[16,32,128]{2,1,0:T(8,128)S(1)} copy-done((f32[16,32,128]{2,1,0:T(8,128)S(1)}, f32[16,32,128]{2,1,0:T(8,128)}, u32[]{:S(2)}) %copy-start.4) | copy-done | bytes 262168
  3.5 0.0 copy-start.6
  3.5 0.9 %copy-done.6 = f32[16,32,128]{2,1,0:T(8,128)S(1)} copy-done((f32[16,32,128]{2,1,0:T(8,128)S(1)}, f32[16,32,128]{2,1,0:T(8,128)}, u32[]{:S(2)}) %copy-start.6) | copy-done | bytes 262168
  4.4 0.0 copy-start.8
  4.4 0.7 %copy-done.8 = s32[32,128]{1,0:T(8,128)S(1)} copy-done((s32[32,128]{1,0:T(8,128)S(1)}, s32[32,128]{1,0:T(8,128)}, u32[]{:S(2)}) %copy-start.8) | copy-done | bytes 16408
  5.2 0.0 copy-start.10
  5.2 0.7 %copy-done.10 = s32[32,128]{1,0:T(8,128)S(1)} copy-done((s32[32,128]{1,0:T(8,128)S(1)}, s32[32,128]{1,0:T(8,128)}, u32[]{:S(2)}) %copy-start.10) | copy-done | bytes 16408
  5.9 0.0 copy-start.12
  5.9 0.0 copy-start.3
  5.9 0.0 copy-start.5
  5.9 0.0 copy-start.7
  5.9 0.0 copy-start.9
  5.9 0.0 copy-start.11
  5.9 0.6 %shard_map.102 = (f32[136,128]{1,0:T(8,128)S(1)}, f32[136,128]{1,0:T(8,128)S(1)}, f32[4,32,128]{2,1,0:T(8,128)S(1)}, f32[40,128]{1,0:T(8,128)S(1)}, f32[40,128]{1,0:T(8,128)S(1)}) custom-call(f32[16,32,128]{2,1,0:T(8,128)S(1)} %copy-done, f32[16,32,128]{2,1,0:T(8,128)S(1)} %copy-done.2, f32[16,32,128]{2,1,0:T(8,128)S(1)} %copy-done.4, ...), custom_call_target="tpu_custom_call" | custom-call | tf_op jit(solution)/shard_map/pallas_call | solution.py:414
  6.5 0.0 copy-start.1
  6.6 4.0 %collective-permute-start = (f32[136,128]{1,0:T(8,128)S(1)}, f32[136,128]{1,0:T(8,128)S(1)}, u32[]{:S(2)}, u32[]{:S(2)}) collective-permute-start(f32[136,128]{1,0:T(8,128)S(1)} %get-tuple-element.13), channel_id=1, source_target_pairs={{0,16},{1,17},{2,18},{3,19},{4,20},{5,21},{6,22},{7,23},{8,24},{9,... | collective-permute-start | bytes 208904 | tf_op jit(solution)/shard_map/ppermute | solution.py:55
  10.5 12.4 %collective-permute-start.1 = (f32[136,128]{1,0:T(8,128)S(1)}, f32[136,128]{1,0:T(8,128)S(1)}, u32[]{:S(2)}, u32[]{:S(2)}) collective-permute-start(f32[136,128]{1,0:T(8,128)S(1)} %get-tuple-element.14), channel_id=1, source_target_pairs={{16,32},{17,33},{18,34},{19,35},{20,36},{21,37},{22,38},{23,39},{2... | collective-permute-start | bytes 208904 | tf_op jit(solution)/shard_map/ppermute | solution.py:55
  22.9 1.9 %collective-permute-start.2 = (f32[8,128]{1,0:T(8,128)S(1)}, f32[8,128]{1,0:T(8,128)S(1)}, u32[]{:S(2)}, u32[]{:S(2)}) collective-permute-start(f32[8,128]{1,0:T(8,128)S(1)} %slice.19), channel_id=1, source_target_pairs={{112,130},{113,143},{114,132},{115,129},{116,134},{117,131},{118,1... | collective-permute-start | bytes 12296 | tf_op jit(solution)/shard_map/ppermute | solution.py:55
  24.8 7.8 %collective-permute-done.2.near_corner = f32[8,128]{1,0:T(8,128)S(1)} collective-permute-done((f32[8,128]{1,0:T(8,128)S(1)}, f32[8,128]{1,0:T(8,128)S(1)}, u32[]{:S(2)}, u32[]{:S(2)}) %collective-permute-start.2) | collective-permute-done | bytes 4128 | tf_op jit(solution)/shard_map/ppermute | solution.py:55
  32.6 0.0 collective-permute-done.even
  32.6 0.0 collective-permute-done.1.odd
  32.7 1.9 %collective-permute-start.3 = (f32[48,128]{1,0:T(8,128)S(1)}, f32[48,128]{1,0:T(8,128)S(1)}, u32[]{:S(2)}, u32[]{:S(2)}) collective-permute-start(f32[48,128]{1,0:T(8,128)S(1)} %get-tuple-element.17), channel_id=1, source_target_pairs={{0,1},{1,0},{2,3},{3,2},{4,5},{5,4},{6,7},{7,6},{8,9},{9,8},{10,11... | collective-permute-start | bytes 73736 | tf_op jit(solution)/shard_map/ppermute | solution.py:55
  34.6 0.7 %collective-permute-start.4 = (f32[48,128]{1,0:T(8,128)S(1)}, f32[48,128]{1,0:T(8,128)S(1)}, u32[]{:S(2)}, u32[]{:S(2)}) collective-permute-start(f32[48,128]{1,0:T(8,128)S(1)} %get-tuple-element.18), channel_id=1, source_target_pairs={{0,15},{1,2},{2,1},{3,4},{4,3},{5,6},{6,5},{7,8},{8,7},{9,10},{10,... | collective-permute-start | bytes 73736 | tf_op jit(solution)/shard_map/ppermute | solution.py:55
  35.3 5.8 %collective-permute-start.5 = (f32[192,128]{1,0:T(8,128)S(1)}, f32[192,128]{1,0:T(8,128)S(1)}, u32[]{:S(2)}, u32[]{:S(2)}) collective-permute-start(f32[192,128]{1,0:T(8,128)S(1)} %get-tuple-element.19), channel_id=1, source_target_pairs={{112,127},{113,114},{114,113},{115,116},{116,115},{117,118},{118,1... | collective-permute-start | bytes 294920 | tf_op jit(solution)/shard_map/ppermute | solution.py:55
  41.1 0.0 copy-done.12
  41.2 0.1 slice.17
  41.3 0.1 slice.18
  41.3 0.1 concatenate.7
  41.4 0.0 collective-permute-done.3.near
  41.4 0.0 collective-permute-done.4.far
  41.4 10.6 %collective-permute-done.5.far_edge = f32[192,128]{1,0:T(8,128)S(1)} collective-permute-done((f32[192,128]{1,0:T(8,128)S(1)}, f32[192,128]{1,0:T(8,128)S(1)}, u32[]{:S(2)}, u32[]{:S(2)}) %collective-permute-start.5) | collective-permute-done | bytes 98336 | tf_op jit(solution)/shard_map/ppermute | solution.py:55
  52.0 0.1 broadcast_in_dim.2.angles
  52.1 0.0 copy-done.3
  52.1 0.0 copy-done.5
  52.1 0.0 copy-done.7
  52.1 0.0 copy-done.9
  52.1 0.0 copy-done.11
  52.1 0.0 copy-done.1
  52.1 4.4 %shard_map.104 = (f32[16,32,128]{2,1,0:T(8,128)}, f32[16,32,128]{2,1,0:T(8,128)}, f32[16,32,128]{2,1,0:T(8,128)}, f32[16,32,128]{2,1,0:T(8,128)}) custom-call(f32[16,32,128]{2,1,0:T(8,128)S(1)} %copy-done.1, f32[16,32,128]{2,1,0:T(8,128)S(1)} %copy-done.3, f32[16,32,128]{2,1,0:T(8,128)S(1)} %copy-done.5, f32[16,32,128]{2,1,0:T(8,128)S(1)} %copy-done.7, ...), custom_call_target="tpu_custom_call" | custom-call | tf_op jit(solution)/shard_map/pallas_call | solution.py:414
  (5 shorter events, 0.1 us)
Async XLA Ops:
  0.6 1.0 %copy-start = (f32[16,32,128]{2,1,0:T(8,128)S(1)}, f32[16,32,128]{2,1,0:T(8,128)}, u32[]{:S(2)}) copy-start(f32[16,32,128]{2,1,0:T(8,128)} %heat.3) | copy-start | bytes 786436
  1.6 0.9 %copy-start.2 = (f32[16,32,128]{2,1,0:T(8,128)S(1)}, f32[16,32,128]{2,1,0:T(8,128)}, u32[]{:S(2)}) copy-start(f32[16,32,128]{2,1,0:T(8,128)} %salt.3) | copy-start | bytes 786436
  2.5 0.9 %copy-start.4 = (f32[16,32,128]{2,1,0:T(8,128)S(1)}, f32[16,32,128]{2,1,0:T(8,128)}, u32[]{:S(2)}) copy-start(f32[16,32,128]{2,1,0:T(8,128)} %zonal.3) | copy-start | bytes 786436
  3.5 0.9 %copy-start.6 = (f32[16,32,128]{2,1,0:T(8,128)S(1)}, f32[16,32,128]{2,1,0:T(8,128)}, u32[]{:S(2)}) copy-start(f32[16,32,128]{2,1,0:T(8,128)} %merid.3) | copy-start | bytes 786436
  4.4 0.7 %copy-start.8 = (s32[32,128]{1,0:T(8,128)S(1)}, s32[32,128]{1,0:T(8,128)}, u32[]{:S(2)}) copy-start(s32[32,128]{1,0:T(8,128)} %flag.3) | copy-start | bytes 49156
  5.2 0.7 %copy-start.10 = (s32[32,128]{1,0:T(8,128)S(1)}, s32[32,128]{1,0:T(8,128)}, u32[]{:S(2)}) copy-start(s32[32,128]{1,0:T(8,128)} %tally.3) | copy-start | bytes 49156
  5.9 35.2 %copy-start.12 = (s32[34]{0:T(128)S(1)}, s32[34]{0:T(128)}, u32[]{:S(2)}) copy-start(s32[34]{0:T(128)} %constant.29) | copy-start | bytes 412
  5.9 46.2 %copy-start.3 = (f32[16,32,128]{2,1,0:T(8,128)S(1)}, f32[16,32,128]{2,1,0:T(8,128)}, u32[]{:S(2)}) copy-start(f32[16,32,128]{2,1,0:T(8,128)} %salt.3) | copy-start | bytes 786436
  5.9 46.2 %copy-start.5 = (f32[16,32,128]{2,1,0:T(8,128)S(1)}, f32[16,32,128]{2,1,0:T(8,128)}, u32[]{:S(2)}) copy-start(f32[16,32,128]{2,1,0:T(8,128)} %zonal.3) | copy-start | bytes 786436
  5.9 46.2 %copy-start.7 = (f32[16,32,128]{2,1,0:T(8,128)S(1)}, f32[16,32,128]{2,1,0:T(8,128)}, u32[]{:S(2)}) copy-start(f32[16,32,128]{2,1,0:T(8,128)} %merid.3) | copy-start | bytes 786436
  5.9 46.2 %copy-start.9 = (s32[32,128]{1,0:T(8,128)S(1)}, s32[32,128]{1,0:T(8,128)}, u32[]{:S(2)}) copy-start(s32[32,128]{1,0:T(8,128)} %flag.3) | copy-start | bytes 49156
  5.9 46.2 %copy-start.11 = (s32[32,128]{1,0:T(8,128)S(1)}, s32[32,128]{1,0:T(8,128)}, u32[]{:S(2)}) copy-start(s32[32,128]{1,0:T(8,128)} %tally.3) | copy-start | bytes 49156
  6.5 45.6 %copy-start.1 = (f32[16,32,128]{2,1,0:T(8,128)S(1)}, f32[16,32,128]{2,1,0:T(8,128)}, u32[]{:S(2)}) copy-start(f32[16,32,128]{2,1,0:T(8,128)} %heat.3) | copy-start | bytes 786436
  6.6 26.1 %collective-permute-start = (f32[136,128]{1,0:T(8,128)S(1)}, f32[136,128]{1,0:T(8,128)S(1)}, u32[]{:S(2)}, u32[]{:S(2)}) collective-permute-start(f32[136,128]{1,0:T(8,128)S(1)} %get-tuple-element.13), channel_id=1, source_target_pairs={{0,16},{1,17},{2,18},{3,19},{4,20},{5,21},{6,22},{7,23},{8,24},{9,... | collective-permute-start | bytes 208904 | tf_op jit(solution)/shard_map/ppermute | solution.py:55
  10.5 22.1 %collective-permute-start.1 = (f32[136,128]{1,0:T(8,128)S(1)}, f32[136,128]{1,0:T(8,128)S(1)}, u32[]{:S(2)}, u32[]{:S(2)}) collective-permute-start(f32[136,128]{1,0:T(8,128)S(1)} %get-tuple-element.14), channel_id=1, source_target_pairs={{16,32},{17,33},{18,34},{19,35},{20,36},{21,37},{22,38},{23,39},{2... | collective-permute-start | bytes 208904 | tf_op jit(solution)/shard_map/ppermute | solution.py:55
  22.9 9.7 %collective-permute-start.2 = (f32[8,128]{1,0:T(8,128)S(1)}, f32[8,128]{1,0:T(8,128)S(1)}, u32[]{:S(2)}, u32[]{:S(2)}) collective-permute-start(f32[8,128]{1,0:T(8,128)S(1)} %slice.19), channel_id=1, source_target_pairs={{112,130},{113,143},{114,132},{115,129},{116,134},{117,131},{118,1... | collective-permute-start | bytes 12296 | tf_op jit(solution)/shard_map/ppermute | solution.py:55
  32.7 8.8 %collective-permute-start.3 = (f32[48,128]{1,0:T(8,128)S(1)}, f32[48,128]{1,0:T(8,128)S(1)}, u32[]{:S(2)}, u32[]{:S(2)}) collective-permute-start(f32[48,128]{1,0:T(8,128)S(1)} %get-tuple-element.17), channel_id=1, source_target_pairs={{0,1},{1,0},{2,3},{3,2},{4,5},{5,4},{6,7},{7,6},{8,9},{9,8},{10,11... | collective-permute-start | bytes 73736 | tf_op jit(solution)/shard_map/ppermute | solution.py:55
  34.6 6.8 %collective-permute-start.4 = (f32[48,128]{1,0:T(8,128)S(1)}, f32[48,128]{1,0:T(8,128)S(1)}, u32[]{:S(2)}, u32[]{:S(2)}) collective-permute-start(f32[48,128]{1,0:T(8,128)S(1)} %get-tuple-element.18), channel_id=1, source_target_pairs={{0,15},{1,2},{2,1},{3,4},{4,3},{5,6},{6,5},{7,8},{8,7},{9,10},{10,... | collective-permute-start | bytes 73736 | tf_op jit(solution)/shard_map/ppermute | solution.py:55
  35.3 16.8 %collective-permute-start.5 = (f32[192,128]{1,0:T(8,128)S(1)}, f32[192,128]{1,0:T(8,128)S(1)}, u32[]{:S(2)}, u32[]{:S(2)}) collective-permute-start(f32[192,128]{1,0:T(8,128)S(1)} %get-tuple-element.19), channel_id=1, source_target_pairs={{112,127},{113,114},{114,113},{115,116},{116,115},{117,118},{118,1... | collective-permute-start | bytes 294920 | tf_op jit(solution)/shard_map/ppermute | solution.py:55

commit v2 on v1

--- a/solution.py
+++ b/solution.py
@@ -16,7 +16,8 @@
 BLOCK = 8
 ROW_MSG = 136
 COL_MSG = 48
-EDGE_MSG = COL_MSG + ROW_MSG + 8
+CHUNK = 4
+EDGE_MSG = COL_MSG + ROW_MSG
 
 
 def near_lon(lat, lon):
@@ -41,11 +42,15 @@
     return lat > 0 and lat % BLOCK in (0, BLOCK - 1)
 
 
+def upper(lon):
+    return lon // 2 % 2 == 1
+
+
 def pairs(where_to, member):
     found = []
     for lat in range(N_LAT):
         for lon in range(N_LON):
-            if member(lat):
+            if member(lat, lon):
                 to_lat, to_lon = where_to(lat, lon)
                 found.append((lat * N_LON + lon, to_lat * N_LON + to_lon))
     return found
@@ -60,10 +65,6 @@
     return far_lon(*to) if is_edge(lat) else to
 
 
-def near_corner_relay(lat, lon):
-    return far_lon(*near_lon(*odd_lat(lat, lon)))
-
-
 def shift(x, by, axis=1):
     by = by % x.shape[axis]
     return x if by == 0 else pltpu.roll(x, by, axis)
@@ -77,10 +78,31 @@
     return lax.axis_index("lat"), lax.axis_index("lon")
 
 
-def pack_kernel(heat, salt, zonal, merid, flag, tally, row_even, row_odd, packed, col_near, col_far):
+def is_upper(lon):
+    return lax.rem(lax.div(lon, 2), 2) == 1
+
+
+def pack_kernel(
+    heat_in, salt_in, zonal_in, merid_in, flag_in, tally_in,
+    row_even, row_odd, packed, col_near, col_far,
+    heat, salt, zonal, merid, flag, tally, sems,
+):
+    copies = [
+        pltpu.make_async_copy(source, held, sems.at[i])
+        for i, (source, held) in enumerate(
+            (
+                (flag_in, flag), (tally_in, tally), (heat_in, heat),
+                (salt_in, salt), (zonal_in, zonal), (merid_in, merid),
+            )
+        )
+    ]
+    for copy in copies:
+        copy.start()
     lat, lon = position()
     lat_odd = lax.rem(lat, 2) == 1
     lon_odd = lax.rem(lon, 2) == 1
+    copies[0].wait()
+    copies[1].wait()
     depth = (flag[...] * tally[...]).astype(jnp.float32)
     lane = lanes_of((ROWS, LANES))
     group = lane >> 3
@@ -88,6 +110,7 @@
     west = jnp.zeros((ROWS, LANES), jnp.float32)
     east = west
     for f, field in enumerate((heat, salt, zonal, merid)):
+        copies[2 + f].wait()
         acc = jnp.zeros((ROWS, LANES), jnp.float32)
         for k in range(LEVELS):
             acc = jnp.where(group == k, shift(field[k], 8 * k + 2), acc)
@@ -118,28 +141,38 @@
     row_odd[128:136, :] = jnp.where(lat_odd, tops, bottoms)
 
 
-def relay_kernel(even, odd, near_corner, col_near, col_far, to_near, to_far, to_far_edge):
+def join_kernel(row_even, row_odd, near, low_out, odd_out, up_out):
+    lat, _ = position()
+    lat_odd = lax.rem(lat, 2) == 1
+    blank = jnp.zeros((2, LANES), jnp.float32)
+    top = jnp.concatenate([near[31:32, :], shift(near[39:40, :], -6), blank], 0)
+    bottom = jnp.concatenate([near[0:1, :], near[32:33, :], blank], 0)
+    low_out[0:132, :] = row_even[0:132, :]
+    up_out[0:132, :] = row_even[0:132, :]
+    odd_out[0:132, :] = row_odd[0:132, :]
+    low_out[132:136, :] = jnp.where(lat_odd, bottom, top)
+    up_out[132:136, :] = jnp.where(lat_odd, bottom, top)
+    odd_out[132:136, :] = jnp.where(lat_odd, top, bottom)
+
+
+def relay_kernel(even_low, odd, even_up, col_far, to_far, to_far_edge):
     _, lon = position()
     lon_odd = lax.rem(lon, 2) == 1
+    info_even = jnp.where(is_upper(lon), even_up[128:136, :], even_low[128:136, :])
+    info_odd = odd[128:136, :]
     blank = jnp.zeros((4, LANES), jnp.float32)
-    info_even = even[128:136, :]
-    info_odd = odd[128:136, :]
 
     def corners(row):
         return jnp.concatenate(
             [info_even[row : row + 1], info_odd[row : row + 1], info_even[0:1], info_odd[0:1], blank], 0
         )
 
-    west, east = corners(2), corners(3)
-    to_near[0:40, :] = col_near[...]
-    to_near[40:48, :] = jnp.where(lon_odd, west, east)
-    far_tile = jnp.where(lon_odd, east, west)
+    far_tile = jnp.where(lon_odd, corners(3), corners(2))
     to_far[0:40, :] = col_far[...]
     to_far[40:48, :] = far_tile
     to_far_edge[0:40, :] = col_far[...]
     to_far_edge[40:48, :] = far_tile
     to_far_edge[48:184, :] = odd[...]
-    to_far_edge[184:192, :] = near_corner[...]
 
 
 def reversed_lanes(x):
@@ -184,8 +217,8 @@
 
 
 def step_kernel(
-    heat, salt, zonal, merid, flag, tally, packed, angles, even, odd, near, far, far_edge,
-    heat_out, salt_out, zonal_out, merid_out, mid,
+    heat, salt, zonal, merid, flag, tally, packed, angles, even_low, odd, even_up, near, far, far_edge,
+    heat_out, salt_out, zonal_out, merid_out, mid, last, sems,
 ):
     lat, lon = position()
     lat_odd = lax.rem(lat, 2) == 1
@@ -207,45 +240,50 @@
     def swap_pair(x):
         return jnp.where(lane1 & 1 == 1, shift(x, 1), shift(x, -1)) * signs
 
-    def unfold_info(info):
-        drow, west, east = info[0:1], info[2:3], info[3:4]
-        return (
-            jnp.where(at_top, reversed_lanes(drow), drow),
-            jnp.where(at_top, swap_pair(east), west),
-            jnp.where(at_top, swap_pair(west), east),
-        )
-
     odd_rows = jnp.where(edge, far_edge[48:184, :], odd[...])
+    beside = odd_rows[132:134]
     turned = reversed_lanes(odd_rows)
     row_field = (lax.broadcasted_iota(jnp.int32, (ROW_MSG, LANES), 0) >> 4) & 3
     below = lax.broadcasted_iota(jnp.int32, (ROW_MSG, LANES), 0) < 128
     turned = jnp.where(jnp.logical_and(below, row_field >= 2), -turned, turned)
     odd_rows = jnp.where(at_top, turned, odd_rows)
-    even_rows = even[...]
+    even_rows = jnp.where(is_upper(lon), even_up[...], even_low[...])
     south_rows = jnp.where(lat_odd, even_rows, odd_rows)
     north_rows = jnp.where(lat_odd, odd_rows, even_rows)
     far_cols = jnp.where(edge, far_edge[0:48, :], far[...])
     near_cols = near[...]
-    west_cols = jnp.where(lon_odd, near_cols, far_cols)
-    east_cols = jnp.where(lon_odd, far_cols, near_cols)
-
-    q_depth, q_west, q_east = unfold_info(odd[128:136, :])
-    s_depth, s_west, s_east = unfold_info(far_edge[184:192, :])
-    far_corner = jnp.where(lon_odd, q_west, q_east)
-    near_corner = jnp.where(lon_odd, s_east, s_west)
-    west_odd = jnp.where(edge, jnp.where(lon_odd, near_corner, far_corner), west_cols[41:42])
-    east_odd = jnp.where(edge, jnp.where(lon_odd, far_corner, near_corner), east_cols[41:42])
-    west_odd_depth = jnp.where(edge, jnp.where(lon_odd, s_depth, q_depth), west_cols[43:44])
-    east_odd_depth = jnp.where(edge, jnp.where(lon_odd, q_depth, s_depth), east_cols[43:44])
+    west_cols = jnp.where(lon_odd, near_cols, far_cols[0:40])
+    east_cols = jnp.where(lon_odd, far_cols[0:40], near_cols)
+
+    q = odd[128:136, :]
+    q_west = jnp.where(at_top, swap_pair(q[3:4]), q[2:3])
+    q_east = jnp.where(at_top, swap_pair(q[2:3]), q[3:4])
+    q_depth = jnp.where(at_top, reversed_lanes(q[0:1]), q[0:1])
+    far_even = far_cols[40:41]
+    far_odd = jnp.where(edge, jnp.where(lon_odd, q_west, q_east), far_cols[41:42])
+    far_odd_d = jnp.where(edge, q_depth, far_cols[43:44])
+    near_even, near_even_d = even_rows[132:133], even_rows[133:134]
+    near_odd = jnp.where(at_top, swap_pair(beside[0:1]), beside[0:1])
+    near_odd_d = jnp.where(at_top, jnp.where(lane1 == 0, shift(beside[1:2], -1), shift(beside[1:2], 1)), beside[1:2])
+
+    def near_depth(row):
+        return jnp.where(lon_odd, row[:, 1:2], row[:, 0:1])
+
+    def far_depth(row):
+        return jnp.where(lon_odd, row[:, 0:1], row[:, 127:128])
 
     def by_side(even_part, odd_part):
         return jnp.where(lat_odd, even_part, odd_part), jnp.where(lat_odd, odd_part, even_part)
 
-    sw, nw = by_side(west_cols[40:41], west_odd)
-    se, ne = by_side(east_cols[40:41], east_odd)
-    sw_d, nw_d = by_side(west_cols[42:43], west_odd_depth)
-    se_d, ne_d = by_side(east_cols[42:43], east_odd_depth)
-    corner_depth = [(x[:, 127:128], y[:, 0:1]) for x, y in ((sw_d, se_d), (nw_d, ne_d))]
+    def west_east(near_part, far_part):
+        return jnp.where(lon_odd, near_part, far_part), jnp.where(lon_odd, far_part, near_part)
+
+    near_s, near_n = by_side(near_even, near_odd)
+    far_s, far_n = by_side(far_even, far_odd)
+    (sw, se), (nw, ne) = west_east(near_s, far_s), west_east(near_n, far_n)
+    near_sd, near_nd = by_side(near_depth(near_even_d), near_depth(near_odd_d))
+    far_sd, far_nd = by_side(far_depth(far_cols[42:43]), far_depth(far_odd_d))
+    corner_depth = [west_east(near_sd, far_sd), west_east(near_nd, far_nd)]
 
     cols, cols_s, cols_n = [], [], []
     for f in range(4):
@@ -392,8 +430,15 @@
 
     outs = (heat_out, salt_out, zonal_out, merid_out)
 
+    copies = []
+
     def to_out(f, k, value):
-        outs[f][k] = value
+        last[f, k] = value
+        if k % CHUNK == CHUNK - 1:
+            part = pl.ds(k + 1 - CHUNK, CHUNK)
+            copy = pltpu.make_async_copy(last.at[f, part], outs[f].at[part], sems.at[f, k // CHUNK])
+            copy.start()
+            copies.append(copy)
 
     whole_step(
         lambda f, k: fields[f][k],
@@ -403,21 +448,23 @@
         to_mid,
     )
     whole_step(lambda f, k: mid[f, k], cols_mid, south_mid, north_mid, to_out)
+    for copy in copies:
+        copy.wait()
 
 
 def shapes(*dims):
     return [jax.ShapeDtypeStruct(d, jnp.float32) for d in dims]
 
 
-def call(kernel, outputs, *operands, scratch=()):
-    vmem = pl.BlockSpec(memory_space=pltpu.VMEM)
+def call(kernel, outputs, *operands, scratch=(), held_in=True, held_out=True, grant=32):
+    vmem, hbm = pl.BlockSpec(memory_space=pltpu.VMEM), pl.BlockSpec(memory_space=pltpu.HBM)
     return pl.pallas_call(
         kernel,
         out_shape=shapes(*outputs),
-        in_specs=[vmem] * len(operands),
-        out_specs=[vmem] * len(outputs),
+        in_specs=[vmem if held_in else hbm] * len(operands),
+        out_specs=[vmem if held_out else hbm] * len(outputs),
         scratch_shapes=list(scratch),
-        compiler_params=pltpu.CompilerParams(vmem_limit_bytes=32 * 1024 * 1024),
+        compiler_params=pltpu.CompilerParams(vmem_limit_bytes=int(grant * 1024 * 1024)),
     )(*operands)
 
 
@@ -434,30 +481,38 @@
 
 def on_device(heat, salt, zonal, merid, flag, tally):
     whole = (heat, salt, zonal, merid, flag, tally)
+    size = (LEVELS, ROWS, LANES)
+    pinned = [pltpu.with_memory_space_constraint(x, pltpu.HBM) for x in whole]
     row_even, row_odd, packed, col_near, col_far = call(
         pack_kernel,
         [(ROW_MSG, LANES), (ROW_MSG, LANES), (4, ROWS, LANES), (40, LANES), (40, LANES)],
-        *whole,
+        *pinned,
+        scratch=[pltpu.VMEM(size, jnp.float32)] * 4
+        + [pltpu.VMEM((ROWS, LANES), jnp.int32)] * 2
+        + [pltpu.SemaphoreType.DMA((6,))],
+        held_in=False,
     )
-    everyone, edges = (lambda lat: True), is_edge
-    corner = send(row_odd[128:136], near_corner_relay, edges)
-    odd = send(row_odd, odd_or_diagonal, lambda lat: lat > 0)
-    even = send(row_even, even_lat, everyone)
-    to_near, to_far, to_far_edge = call(
-        relay_kernel,
-        [(COL_MSG, LANES), (COL_MSG, LANES), (EDGE_MSG, LANES)],
-        even, odd, corner, col_near, col_far,
+    near = send(col_near, near_lon, lambda lat, lon: True)
+    row_low, row_odd, row_up = call(join_kernel, [(ROW_MSG, LANES)] * 3, row_even, row_odd, near)
+    even_low = send(row_low, even_lat, lambda lat, lon: not upper(lon))
+    odd = send(row_odd, odd_or_diagonal, lambda lat, lon: lat > 0)
+    even_up = send(row_up, even_lat, lambda lat, lon: upper(lon))
+    to_far, to_far_edge = call(
+        relay_kernel, [(COL_MSG, LANES), (EDGE_MSG, LANES)], even_low, odd, even_up, col_far
     )
-    far_edge = send(to_far_edge, far_lon, edges)
-    far = send(to_far, far_lon, lambda lat: not is_edge(lat))
-    near = send(to_near, near_lon, everyone)
-    size = (LEVELS, ROWS, LANES)
+    far = send(to_far, far_lon, lambda lat, lon: not is_edge(lat))
+    far_edge = send(to_far_edge, far_lon, lambda lat, lon: is_edge(lat))
     return tuple(
         call(
             step_kernel,
             [size] * 4,
-            *whole, packed, angle_table(), even, odd, near, far, far_edge,
-            scratch=[pltpu.VMEM((4,) + size, jnp.float32)],
+            *whole, packed, angle_table(), even_low, odd, even_up, near, far, far_edge,
+            scratch=[
+                pltpu.VMEM((4,) + size, jnp.float32),
+                pltpu.VMEM((4,) + size, jnp.float32),
+                pltpu.SemaphoreType.DMA((4, LEVELS // CHUNK)),
+            ],
+            held_out=False,
         )
     )
 

time: 57 us -> 45 us (0.79)
  waiting for transfers between devices: 18.4 us -> 7.48 us
  local copies, waits for them, and re-layouts: 5.6 us -> 0.37 us
  starting transfers between devices: 26.7 us -> 29.5 us
  Pallas kernels: 5.08 us -> 6.43 us
    ppermute x6, waiting for transfers between devices: 18.4 us -> 7.48 us  [send(): return lax.ppermute(array, ('lat', 'lon'), pairs(where_to, member))]
    unnamed x26 -> x14, local copies, waits for them, and re-layouts: 5.26 us -> 0.03 us
    ppermute x6, starting transfers between devices: 26.7 us -> 29.5 us  [send(): return lax.ppermute(array, ('lat', 'lon'), pairs(where_to, member))]
    pallas_call x3 -> x4, Pallas kernels: 5.08 us -> 6.43 us  [call(): pl.pallas_call(kernel, out_shape=shapes(*outputs), in_specs=[vmem if held...]
  transfers between devices with their start and end apart: 6 -> 6, of which waited for: 2 -> 3; matrix products, arithmetic and copies ran while one was open for 1% -> 1% of each run, Pallas kernels for 0% -> 0%
where the time goes in v2:
time: 45 us; the launch traced here: 44.7 us
  starting transfers between devices  29.5 us (66%)
  waiting for transfers between devices  7.48 us (17%)
  Pallas kernels  6.43 us (14%)
  between operations  0.81 us (2%)
    ppermute x6, starting transfers between devices, send(): return lax.ppermute(array, ('lat', 'lon'), pairs(where_to, member))  29.5 us
    ppermute x6, waiting for transfers between devices, send(): return lax.ppermute(array, ('lat', 'lon'), pairs(where_to, member))  7.48 us
    pallas_call x4, Pallas kernels, call(): pl.pallas_call(kernel, out_shape=shapes(*outputs), in_specs=[vmem if held...  6.43 us
  transfers between devices with their start and end apart: 6, of which 3 were waited for; matrix products, arithmetic and copies ran while one was open for 1% of the time, Pallas kernels for 0%

profile of v2, /device:TPU:6, one launch (start us, length us, event | category | flops | bytes accessed | tf_op | source)
XLA Modules:
  0.0 44.7 jit_solution(9616526655511805421)
XLA Ops:
  0.6 0.0 copy-start.1
  0.6 0.0 copy-start.2
  0.7 0.0 copy-start.3
  0.7 2.0 %shard_map.102 = (f32[136,128]{1,0:T(8,128)S(1)}, f32[136,128]{1,0:T(8,128)S(1)}, f32[4,32,128]{2,1,0:T(8,128)S(1)}, f32[40,128]{1,0:T(8,128)S(1)}, f32[40,128]{1,0:T(8,128)S(1)}) custom-call(f32[16,32,128]{2,1,0:T(8,128)} %heat.1, f32[16,32,128]{2,1,0:T(8,128)} %salt.1, f32[16,32,128]{2,1,0:T(8,128)} %zonal.1, f32[16,32,128]{2,1,0:T(8,128)} %merid.1, ...), custom_call_target="tpu_custom_call" | custom-call | tf_op jit(solution)/shard_map/pallas_call | solution.py:461
  2.6 0.0 copy-start
  2.6 2.1 %collective-permute-start = (f32[40,128]{1,0:T(8,128)S(1)}, f32[40,128]{1,0:T(8,128)S(1)}, u32[]{:S(2)}, u32[]{:S(2)}) collective-permute-start(f32[40,128]{1,0:T(8,128)S(1)} %get-tuple-element.17), channel_id=1, source_target_pairs={{0,1},{1,0},{2,3},{3,2},{4,5},{5,4},{6,7},{7,6},{8,9},{9,8},{10,11... | collective-permute-start | bytes 61448 | tf_op jit(solution)/shard_map/ppermute | solution.py:60
  4.7 1.2 %collective-permute-done.near = f32[40,128]{1,0:T(8,128)S(1)} collective-permute-done((f32[40,128]{1,0:T(8,128)S(1)}, f32[40,128]{1,0:T(8,128)S(1)}, u32[]{:S(2)}, u32[]{:S(2)}) %collective-permute-start) | collective-permute-done | bytes 20512 | tf_op jit(solution)/shard_map/ppermute | solution.py:60
  5.9 0.1 shard_map.103
  5.9 3.8 %collective-permute-start.1 = (f32[136,128]{1,0:T(8,128)S(1)}, f32[136,128]{1,0:T(8,128)S(1)}, u32[]{:S(2)}, u32[]{:S(2)}) collective-permute-start(f32[136,128]{1,0:T(8,128)S(1)} %get-tuple-element.18), channel_id=1, source_target_pairs={{0,16},{1,17},{4,20},{5,21},{8,24},{9,25},{12,28},{13,29},{16,0},{... | collective-permute-start | bytes 208904 | tf_op jit(solution)/shard_map/ppermute | solution.py:60
  9.8 10.7 %collective-permute-start.2 = (f32[136,128]{1,0:T(8,128)S(1)}, f32[136,128]{1,0:T(8,128)S(1)}, u32[]{:S(2)}, u32[]{:S(2)}) collective-permute-start(f32[136,128]{1,0:T(8,128)S(1)} %get-tuple-element.19), channel_id=1, source_target_pairs={{16,32},{17,33},{18,34},{19,35},{20,36},{21,37},{22,38},{23,39},{2... | collective-permute-start | bytes 208904 | tf_op jit(solution)/shard_map/ppermute | solution.py:60
  20.5 0.7 %collective-permute-start.3 = (f32[136,128]{1,0:T(8,128)S(1)}, f32[136,128]{1,0:T(8,128)S(1)}, u32[]{:S(2)}, u32[]{:S(2)}) collective-permute-start(f32[136,128]{1,0:T(8,128)S(1)} %get-tuple-element.20), channel_id=1, source_target_pairs={{2,18},{3,19},{6,22},{7,23},{10,26},{11,27},{14,30},{15,31},{18,2}... | collective-permute-start | bytes 208904 | tf_op jit(solution)/shard_map/ppermute | solution.py:60
  21.2 0.0 collective-permute-done.1.even_low
  21.2 1.6 %collective-permute-done.2.odd = f32[136,128]{1,0:T(8,128)S(1)} collective-permute-done((f32[136,128]{1,0:T(8,128)S(1)}, f32[136,128]{1,0:T(8,128)S(1)}, u32[]{:S(2)}, u32[]{:S(2)}) %collective-permute-start.2) | collective-permute-done | bytes 69664 | tf_op jit(solution)/shard_map/ppermute | solution.py:60
  22.8 0.0 collective-permute-done.3.even_up
  22.8 0.0 copy-start.6
  22.8 0.7 %collective-permute-start.4 = (f32[48,128]{1,0:T(8,128)S(1)}, f32[48,128]{1,0:T(8,128)S(1)}, u32[]{:S(2)}, u32[]{:S(2)}) collective-permute-start(f32[48,128]{1,0:T(8,128)S(1)} %get-tuple-element.22), channel_id=1, source_target_pairs={{0,15},{1,2},{2,1},{3,4},{4,3},{5,6},{6,5},{7,8},{8,7},{9,10},{10,... | collective-permute-start | bytes 73736 | tf_op jit(solution)/shard_map/ppermute | solution.py:60
  23.5 11.6 %collective-permute-start.5 = (f32[184,128]{1,0:T(8,128)S(1)}, f32[184,128]{1,0:T(8,128)S(1)}, u32[]{:S(2)}, u32[]{:S(2)}) collective-permute-start(f32[184,128]{1,0:T(8,128)S(1)} %get-tuple-element.23), channel_id=1, source_target_pairs={{112,127},{113,114},{114,113},{115,116},{116,115},{117,118},{118,1... | collective-permute-start | bytes 282632 | tf_op jit(solution)/shard_map/ppermute | solution.py:60
  35.1 0.0 copy-done.6
  35.2 0.1 slice.14
  35.3 0.1 slice.15
  35.4 0.1 concatenate.7
  35.4 0.0 copy-start.4
  35.4 0.0 copy-start.5
  35.4 0.0 collective-permute-done.4.far
  35.5 4.7 %collective-permute-done.5.far_edge = f32[184,128]{1,0:T(8,128)S(1)} collective-permute-done((f32[184,128]{1,0:T(8,128)S(1)}, f32[184,128]{1,0:T(8,128)S(1)}, u32[]{:S(2)}, u32[]{:S(2)}) %collective-permute-start.5) | collective-permute-done | bytes 94240 | tf_op jit(solution)/shard_map/ppermute | solution.py:60
  40.2 0.1 broadcast_in_dim.2.angles
  40.3 0.0 copy-done.1
  40.3 0.0 copy-done.2
  40.3 0.0 copy-done.3
  40.3 0.0 copy-done
  40.3 0.0 copy-done.4
  40.3 0.0 copy-done.5
  40.3 4.4 %shard_map.105 = (f32[16,32,128]{2,1,0:T(8,128)}, f32[16,32,128]{2,1,0:T(8,128)}, f32[16,32,128]{2,1,0:T(8,128)}, f32[16,32,128]{2,1,0:T(8,128)}) custom-call(f32[16,32,128]{2,1,0:T(8,128)S(1)} %copy-done, f32[16,32,128]{2,1,0:T(8,128)S(1)} %copy-done.1, f32[16,32,128]{2,1,0:T(8,128)S(1)} %copy-done.2, f32[16,32,128]{2,1,0:T(8,128)S(1)} %copy-done.3, ...), custom_call_target="tpu_custom_call" | custom-call | tf_op jit(solution)/shard_map/pallas_call | solution.py:461
  (4 shorter events, 0.1 us)
Async XLA Ops:
  0.6 39.6 %copy-start.1 = (f32[16,32,128]{2,1,0:T(8,128)S(1)}, f32[16,32,128]{2,1,0:T(8,128)}, u32[]{:S(2)}) copy-start(f32[16,32,128]{2,1,0:T(8,128)} %salt.1) | copy-start | bytes 786436
  0.6 39.6 %copy-start.2 = (f32[16,32,128]{2,1,0:T(8,128)S(1)}, f32[16,32,128]{2,1,0:T(8,128)}, u32[]{:S(2)}) copy-start(f32[16,32,128]{2,1,0:T(8,128)} %zonal.1) | copy-start | bytes 786436
  0.7 39.6 %copy-start.3 = (f32[16,32,128]{2,1,0:T(8,128)S(1)}, f32[16,32,128]{2,1,0:T(8,128)}, u32[]{:S(2)}) copy-start(f32[16,32,128]{2,1,0:T(8,128)} %merid.1) | copy-start | bytes 786436
  2.6 37.6 %copy-start = (f32[16,32,128]{2,1,0:T(8,128)S(1)}, f32[16,32,128]{2,1,0:T(8,128)}, u32[]{:S(2)}) copy-start(f32[16,32,128]{2,1,0:T(8,128)} %heat.1) | copy-start | bytes 786436
  2.6 3.2 %collective-permute-start = (f32[40,128]{1,0:T(8,128)S(1)}, f32[40,128]{1,0:T(8,128)S(1)}, u32[]{:S(2)}, u32[]{:S(2)}) collective-permute-start(f32[40,128]{1,0:T(8,128)S(1)} %get-tuple-element.17), channel_id=1, source_target_pairs={{0,1},{1,0},{2,3},{3,2},{4,5},{5,4},{6,7},{7,6},{8,9},{9,8},{10,11... | collective-permute-start | bytes 61448 | tf_op jit(solution)/shard_map/ppermute | solution.py:60
  5.9 15.2 %collective-permute-start.1 = (f32[136,128]{1,0:T(8,128)S(1)}, f32[136,128]{1,0:T(8,128)S(1)}, u32[]{:S(2)}, u32[]{:S(2)}) collective-permute-start(f32[136,128]{1,0:T(8,128)S(1)} %get-tuple-element.18), channel_id=1, source_target_pairs={{0,16},{1,17},{4,20},{5,21},{8,24},{9,25},{12,28},{13,29},{16,0},{... | collective-permute-start | bytes 208904 | tf_op jit(solution)/shard_map/ppermute | solution.py:60
  9.8 13.0 %collective-permute-start.2 = (f32[136,128]{1,0:T(8,128)S(1)}, f32[136,128]{1,0:T(8,128)S(1)}, u32[]{:S(2)}, u32[]{:S(2)}) collective-permute-start(f32[136,128]{1,0:T(8,128)S(1)} %get-tuple-element.19), channel_id=1, source_target_pairs={{16,32},{17,33},{18,34},{19,35},{20,36},{21,37},{22,38},{23,39},{2... | collective-permute-start | bytes 208904 | tf_op jit(solution)/shard_map/ppermute | solution.py:60
  20.5 2.3 %collective-permute-start.3 = (f32[136,128]{1,0:T(8,128)S(1)}, f32[136,128]{1,0:T(8,128)S(1)}, u32[]{:S(2)}, u32[]{:S(2)}) collective-permute-start(f32[136,128]{1,0:T(8,128)S(1)} %get-tuple-element.20), channel_id=1, source_target_pairs={{2,18},{3,19},{6,22},{7,23},{10,26},{11,27},{14,30},{15,31},{18,2}... | collective-permute-start | bytes 208904 | tf_op jit(solution)/shard_map/ppermute | solution.py:60
  22.8 12.3 %copy-start.6 = (s32[34]{0:T(128)S(1)}, s32[34]{0:T(128)}, u32[]{:S(2)}) copy-start(s32[34]{0:T(128)} %constant.29) | copy-start | bytes 412
  22.8 12.6 %collective-permute-start.4 = (f32[48,128]{1,0:T(8,128)S(1)}, f32[48,128]{1,0:T(8,128)S(1)}, u32[]{:S(2)}, u32[]{:S(2)}) collective-permute-start(f32[48,128]{1,0:T(8,128)S(1)} %get-tuple-element.22), channel_id=1, source_target_pairs={{0,15},{1,2},{2,1},{3,4},{4,3},{5,6},{6,5},{7,8},{8,7},{9,10},{10,... | collective-permute-start | bytes 73736 | tf_op jit(solution)/shard_map/ppermute | solution.py:60
  23.5 16.7 %collective-permute-start.5 = (f32[184,128]{1,0:T(8,128)S(1)}, f32[184,128]{1,0:T(8,128)S(1)}, u32[]{:S(2)}, u32[]{:S(2)}) collective-permute-start(f32[184,128]{1,0:T(8,128)S(1)} %get-tuple-element.23), channel_id=1, source_target_pairs={{112,127},{113,114},{114,113},{115,116},{116,115},{117,118},{118,1... | collective-permute-start | bytes 282632 | tf_op jit(solution)/shard_map/ppermute | solution.py:60
  35.4 4.9 %copy-start.4 = (s32[32,128]{1,0:T(8,128)S(1)}, s32[32,128]{1,0:T(8,128)}, u32[]{:S(2)}) copy-start(s32[32,128]{1,0:T(8,128)} %flag.1) | copy-start | bytes 49156
  35.4 4.9 %copy-start.5 = (s32[32,128]{1,0:T(8,128)S(1)}, s32[32,128]{1,0:T(8,128)}, u32[]{:S(2)}) copy-start(s32[32,128]{1,0:T(8,128)} %tally.1) | copy-start | bytes 49156

commit v3 on v2

v3 whole, which is shorter than its diff:
```python
import jax
import jax.numpy as jnp
from jax import lax
from jax.experimental import pallas as pl
from jax.experimental.pallas import tpu as pltpu
from jax.sharding import PartitionSpec as P

MIXING = 0.2
VISCOSITY = 0.05
ROTATION = 0.3
LEVELS = 16
ROWS = 32
LANES = 128
N_LAT = 32
N_LON = 16
BLOCK = 8
ROW_MSG = 136
COL_MSG = 48
CHUNK = 4
EDGE_MSG = COL_MSG + ROW_MSG


def near_lon(lat, lon):
    return lat, lon ^ 1


def far_lon(lat, lon):
    return lat, (lon + 1) % N_LON if lon % 2 else (lon - 1) % N_LON


def even_lat(lat, lon):
    return lat ^ 1, lon


def odd_lat(lat, lon):
    if lat == N_LAT - 1:
        return lat, N_LON - 1 - lon
    return (lat + 1 if lat % 2 else lat - 1), lon


def is_edge(lat):
    return lat > 0 and lat % BLOCK in (0, BLOCK - 1)


def upper(lon):
    return lon // 2 % 2 == 1


def pairs(where_to, member):
    found = []
    for lat in range(N_LAT):
        for lon in range(N_LON):
            if member(lat, lon):
                to_lat, to_lon = where_to(lat, lon)
                found.append((lat * N_LON + lon, to_lat * N_LON + to_lon))
    return found


def send(array, where_to, member):
    return lax.ppermute(array, ("lat", "lon"), pairs(where_to, member))


def odd_or_diagonal(lat, lon):
    to = odd_lat(lat, lon)
    return far_lon(*to) if is_edge(lat) else to


def shift(x, by, axis=1):
    by = by % x.shape[axis]
    return x if by == 0 else pltpu.roll(x, by, axis)


def lanes_of(shape):
    return lax.broadcasted_iota(jnp.int32, shape, 1)


def position():
    return lax.axis_index("lat"), lax.axis_index("lon")


def is_upper(lon):
    return lax.rem(lax.div(lon, 2), 2) == 1


def pack_kernel(
    heat_in, salt_in, zonal_in, merid_in, flag_in, tally_in,
    heat, salt, zonal, merid, depth_out, packed, info_top, info_bottom, col_near, col_far,
    flag, tally, sems,
):
    copies = [
        pltpu.make_async_copy(source, held, sems.at[i])
        for i, (source, held) in enumerate(
            (
                (flag_in, flag), (tally_in, tally), (heat_in, heat),
                (salt_in, salt), (zonal_in, zonal), (merid_in, merid),
            )
        )
    ]
    for copy in copies:
        copy.start()
    _, lon = position()
    lon_odd = lax.rem(lon, 2) == 1
    copies[0].wait()
    copies[1].wait()
    depth = (flag[...] * tally[...]).astype(jnp.float32)
    depth_out[...] = depth
    lane = lanes_of((ROWS, LANES))
    group = lane >> 3
    pair = (lane & 7) >> 1
    west = jnp.zeros((ROWS, LANES), jnp.float32)
    east = west
    for f, field in enumerate((heat, salt, zonal, merid)):
        copies[2 + f].wait()
        acc = jnp.zeros((ROWS, LANES), jnp.float32)
        for k in range(LEVELS):
            acc = jnp.where(group == k, shift(field[k], 8 * k + 2), acc)
        packed[f] = acc
        west = jnp.where(pair == f, shift(acc, 2 * f - 2), west)
        east = jnp.where(pair == f, shift(acc, 2 * f), east)
    short = lanes_of((8, LANES)) >> 1
    depth_west = jnp.zeros((8, LANES), jnp.float32)
    depth_east = depth_west
    for i in range(4):
        part = depth[8 * i : 8 * i + 8]
        depth_west = jnp.where(short == i, shift(part, 2 * i), depth_west)
        depth_east = jnp.where(short == i, shift(part, 2 * i + 2), depth_east)
    col_near[0:ROWS, :] = jnp.where(lon_odd, west, east)
    col_far[0:ROWS, :] = jnp.where(lon_odd, east, west)
    col_near[ROWS : ROWS + 8, :] = jnp.where(lon_odd, depth_west, depth_east)
    col_far[ROWS : ROWS + 8, :] = jnp.where(lon_odd, depth_east, depth_west)
    blank = jnp.zeros((4, LANES), jnp.float32)
    info_top[...] = jnp.concatenate([depth[31:32], depth[30:31], west[31:32], east[31:32], blank], 0)
    info_bottom[...] = jnp.concatenate([depth[0:1], depth[1:2], west[0:1], east[0:1], blank], 0)


def row_kernel(heat, salt, zonal, merid, low_out, odd_out, up_out):
    lat, _ = position()
    lat_odd = lax.rem(lat, 2) == 1
    for f, field in enumerate((heat, salt, zonal, merid)):
        for d in range(2):
            at = (d * 4 + f) * LEVELS
            top = field[:, ROWS - 1 - d, :]
            bottom = field[:, d, :]
            even = jnp.where(lat_odd, bottom, top)
            low_out[at : at + LEVELS, :] = even
            up_out[at : at + LEVELS, :] = even
            odd_out[at : at + LEVELS, :] = jnp.where(lat_odd, top, bottom)


def join_kernel(low, odd, up, info_top, info_bottom, near, low_out, odd_out, up_out):
    lat, _ = position()
    lat_odd = lax.rem(lat, 2) == 1
    blank = jnp.zeros((2, LANES), jnp.float32)
    top = jnp.concatenate([info_top[0:4, :], near[31:32, :], shift(near[39:40, :], -6), blank], 0)
    bottom = jnp.concatenate([info_bottom[0:4, :], near[0:1, :], near[32:33, :], blank], 0)
    low_out[0:128, :] = low[...]
    up_out[0:128, :] = up[...]
    odd_out[0:128, :] = odd[...]
    even_info = jnp.where(lat_odd, bottom, top)
    low_out[128:136, :] = even_info
    up_out[128:136, :] = even_info
    odd_out[128:136, :] = jnp.where(lat_odd, top, bottom)


def relay_kernel(even_low, odd, even_up, col_far, to_far, to_far_edge):
    _, lon = position()
    lon_odd = lax.rem(lon, 2) == 1
    info_even = jnp.where(is_upper(lon), even_up[128:136, :], even_low[128:136, :])
    info_odd = odd[128:136, :]
    blank = jnp.zeros((4, LANES), jnp.float32)

    def corners(row):
        return jnp.concatenate(
            [info_even[row : row + 1], info_odd[row : row + 1], info_even[0:1], info_odd[0:1], blank], 0
        )

    far_tile = jnp.where(lon_odd, corners(3), corners(2))
    to_far[0:40, :] = col_far[...]
    to_far[40:48, :] = far_tile
    to_far_edge[0:40, :] = col_far[...]
    to_far_edge[40:48, :] = far_tile
    to_far_edge[48:184, :] = odd[...]


def reversed_lanes(x):
    lane = lanes_of(x.shape)
    for b in range(7):
        x = jnp.where((lane >> b) & 1 == 1, shift(x, 1 << b), shift(x, -(1 << b)))
    return x


def five_point(c, e, w, n, s, up, down, wet, wets, wet_up, wet_down, cosine, sine):
    wet_e, wet_w, wet_n, wet_s = (wet * x for x in wets)
    flow_e = 0.5 * (c[2] + e[2]) * wet_e
    flow_w = 0.5 * (c[2] + w[2]) * wet_w
    flow_n = 0.5 * (c[3] + n[3]) * wet_n
    flow_s = 0.5 * (c[3] + s[3]) * wet_s

    def gain(f, viscosity):
        east = (jnp.maximum(flow_e, 0.0) * c[f] + jnp.minimum(flow_e, 0.0) * e[f]) - viscosity * wet_e * (e[f] - c[f])
        west = (jnp.maximum(flow_w, 0.0) * w[f] + jnp.minimum(flow_w, 0.0) * c[f]) - viscosity * wet_w * (c[f] - w[f])
        north = (jnp.maximum(flow_n, 0.0) * c[f] + jnp.minimum(flow_n, 0.0) * n[f]) - viscosity * wet_n * (n[f] - c[f])
        south = (jnp.maximum(flow_s, 0.0) * s[f] + jnp.minimum(flow_s, 0.0) * c[f]) - viscosity * wet_s * (c[f] - s[f])
        return c[f] - ((east - west) + (north - south))

    def tracer(f):
        mixed = MIXING * ((up[f] - c[f]) * (wet * wet_up) - (c[f] - down[f]) * (wet * wet_down))
        return wet * (gain(f, 0.0) + mixed)

    ua, va = gain(2, VISCOSITY), gain(3, VISCOSITY)
    return [tracer(0), tracer(1), wet * (cosine * ua + sine * va), wet * (cosine * va - sine * ua)]


def north_of(x, last):
    return jnp.concatenate([x[1:], last], 0)


def south_of(x, first):
    return jnp.concatenate([first, x[:-1]], 0)


def as_wet(mask):
    return jnp.where(mask, 1.0, 0.0)


def column_groups(packed, depth, west_cols, east_cols):
    lane = lanes_of((ROWS, LANES))
    place = lane & 7
    cols = []
    for f in range(4):
        own = packed[f]
        x = jnp.where(place < 2, own, shift(own, 4))
        x = jnp.where((place >> 1) == 1, shift(east_cols[0:32], 2 - 2 * f), x)
        cols.append(jnp.where((place >> 1) == 2, shift(west_cols[0:32], 4 - 2 * f), x))
    west_d = jnp.concatenate([shift(west_cols[32:40], 4 - 2 * i) for i in range(4)], 0)
    east_d = jnp.concatenate([shift(east_cols[32:40], 2 - 2 * i) for i in range(4)], 0)
    col_depth = jnp.where(lane < 2, shift(depth, 2), shift(depth, 6))
    col_depth = jnp.where((lane >> 1) == 1, east_d, col_depth)
    col_depth = jnp.where((lane >> 1) == 2, west_d, col_depth)
    col_depth = jnp.where(lane < 8, col_depth, 0.0)
    for b in (8, 16, 32, 64):
        col_depth = col_depth + shift(col_depth, b)
    return cols, col_depth


def depths_beside(depth, col_depth, south, north):
    lane = lanes_of((ROWS, LANES))
    return (
        jnp.where(lane == 127, shift(col_depth, 125), shift(depth, -1)),
        jnp.where(lane == 0, shift(col_depth, 123), shift(depth, 1)),
        north_of(depth, north),
        south_of(depth, south),
    )


def whole_step(read, col_values, rows_s, rows_n, write, depth, beside, cosine, sine):
    lane = lanes_of((ROWS, LANES))
    place = lane & 7
    row = lax.broadcasted_iota(jnp.int32, (ROWS, LANES), 0)
    first_row, last_row = row == 0, row == ROWS - 1
    m_e, m_w, m_n, m_s = (jnp.minimum(depth, x) for x in beside)
    sides = [jnp.where(place == 2, x, shift(x, -2)) for x in col_values]
    now = [read(f, 0) for f in range(4)]
    carried = [None, None]
    for k in range(LEVELS):
        above = [read(f, k + 1) for f in range(4)] if k + 1 < LEVELS else None
        half_e, half_w, half_n, half_s = (jnp.where(k < x, 0.5, 0.0) for x in (m_e, m_w, m_n, m_s))
        e, w, n, s = [], [], [], []
        for f in range(4):
            x = now[f]
            ends = shift(sides[f], 127 - (8 * k + 2))
            e.append(jnp.where(lane == 127, ends, shift(x, -1)))
            w.append(jnp.where(lane == 0, ends, shift(x, 1)))
            n.append(jnp.where(last_row, rows_n[f][k : k + 1], shift(x, -1, 0)))
            s.append(jnp.where(first_row, rows_s[f][k : k + 1], shift(x, 1, 0)))
        flow_e = (now[2] + e[2]) * half_e
        flow_w = (now[2] + w[2]) * half_w
        flow_n = (now[3] + n[3]) * half_n
        flow_s = (now[3] + s[3]) * half_s
        out_e, in_e = jnp.maximum(flow_e, 0.0), jnp.minimum(flow_e, 0.0)
        in_w, out_w = jnp.maximum(flow_w, 0.0), jnp.minimum(flow_w, 0.0)
        out_n, in_n = jnp.maximum(flow_n, 0.0), jnp.minimum(flow_n, 0.0)
        in_s, out_s = jnp.maximum(flow_s, 0.0), jnp.minimum(flow_s, 0.0)
        kept = 1.0 - ((out_e - out_w) + (out_n - out_s))
        wet = k < depth
        new = []
        for f in range(2):
            x = now[f]
            total = (x * kept - (in_e * e[f] - in_w * w[f])) - (in_n * n[f] - in_s * s[f])
            if above is not None:
                flux = jnp.where(k + 1 < depth, MIXING * (above[f] - x), 0.0)
                total = total + flux
            if carried[f] is not None:
                total = total - carried[f]
            if above is not None:
                carried[f] = flux
            new.append(jnp.where(wet, total, 0.0))
        thick = 2.0 * VISCOSITY
        vis_e, vis_w, vis_n, vis_s = (thick * x for x in (half_e, half_w, half_n, half_s))
        kept = kept - ((vis_e + vis_w) + (vis_n + vis_s))
        in_e, in_w, in_n, in_s = vis_e - in_e, vis_w + in_w, vis_n - in_n, vis_s + in_s
        ua, va = (
            (now[f] * kept + (in_e * e[f] + in_w * w[f])) + (in_n * n[f] + in_s * s[f]) for f in (2, 3)
        )
        new.append(jnp.where(wet, cosine * ua + sine * va, 0.0))
        new.append(jnp.where(wet, cosine * va - sine * ua, 0.0))
        for f in range(4):
            write(f, k, new[f])
        now = above


def early_kernel(
    heat, salt, zonal, merid, depth_in, packed, angles, even_low, odd, even_up, near, mid_out
):
    lat, lon = position()
    lat_odd = lax.rem(lat, 2) == 1
    lon_odd = lax.rem(lon, 2) == 1
    fields = (heat, salt, zonal, merid)
    depth = depth_in[...]
    even_rows = jnp.where(is_upper(lon), even_up[...], even_low[...])
    odd_rows = odd[...]
    south_rows = jnp.where(lat_odd, even_rows, odd_rows)
    north_rows = jnp.where(lat_odd, odd_rows, even_rows)
    near_cols = near[...]
    west_cols = jnp.where(lon_odd, near_cols, 0.0)
    east_cols = jnp.where(lon_odd, 0.0, near_cols)
    cols, col_depth = column_groups(packed, depth, west_cols, east_cols)

    def write(f, k, value):
        mid_out[f, k] = value

    whole_step(
        lambda f, k: fields[f][k],
        cols,
        [south_rows[f * 16 : f * 16 + 16] for f in range(4)],
        [north_rows[f * 16 : f * 16 + 16] for f in range(4)],
        write,
        depth,
        depths_beside(depth, col_depth, south_rows[128:129], north_rows[128:129]),
        angles[0:32, :],
        angles[32:64, :],
    )


def step_kernel(
    mid, heat, salt, zonal, merid, depth_in, packed, angles, even_low, odd, even_up, near, far_edge, far,
    heat_out, salt_out, zonal_out, merid_out, turned, last, sems,
):
    lat, lon = position()
    lat_odd = lax.rem(lat, 2) == 1
    lon_odd = lax.rem(lon, 2) == 1
    at_top = lat == N_LAT - 1
    run = lax.rem(lat, BLOCK)
    edge = jnp.logical_and(lat > 0, jnp.logical_or(run == 0, run == BLOCK - 1))
    fields = (heat, salt, zonal, merid)
    lane = lanes_of((ROWS, LANES))
    place = lane & 7
    level = (lane >> 3).astype(jnp.float32)
    lane1 = lanes_of((1, LANES))
    place1 = lane1 & 7
    depth = depth_in[...]
    cosine, sine = angles[0:32, :], angles[32:64, :]

    signs = jnp.where(jnp.logical_and(at_top, place1 >= 4), -1.0, 1.0)

    def swap_pair(x):
        return jnp.where(lane1 & 1 == 1, shift(x, 1), shift(x, -1)) * signs

    odd_rows = jnp.where(edge, far_edge[48:184, :], odd[...])
    beside = odd_rows[132:134]
    turned[...] = odd_rows

    @pl.when(at_top)
    def _():
        for at in range(0, 130, 16):
            part = reversed_lanes(odd_rows[at : min(at + 16, 130)])
            turned[at : min(at + 16, 130), :] = -part if at < 128 and at // 16 % 4 >= 2 else part

    odd_info = odd_rows[130:132]
    odd_rows = turned[...]
    even_rows = jnp.where(is_upper(lon), even_up[...], even_low[...])
    south_rows = jnp.where(lat_odd, even_rows, odd_rows)
    north_rows = jnp.where(lat_odd, odd_rows, even_rows)
    far_cols = jnp.where(edge, far_edge[0:48, :], far[...])
    near_cols = near[...]
    west_cols = jnp.where(lon_odd, near_cols, far_cols[0:40])
    east_cols = jnp.where(lon_odd, far_cols[0:40], near_cols)

    q = odd[128:136, :]
    q_west = jnp.where(at_top, swap_pair(q[3:4]), q[2:3])
    q_east = jnp.where(at_top, swap_pair(q[2:3]), q[3:4])
    q_depth = jnp.where(at_top, reversed_lanes(q[0:1]), q[0:1])
    far_even = far_cols[40:41]
    far_odd = jnp.where(edge, jnp.where(lon_odd, q_west, q_east), far_cols[41:42])
    far_odd_d = jnp.where(edge, q_depth, far_cols[43:44])
    near_even, near_even_d = even_rows[132:133], even_rows[133:134]
    near_odd = jnp.where(at_top, swap_pair(beside[0:1]), beside[0:1])
    near_odd_d = jnp.where(at_top, jnp.where(lane1 == 0, shift(beside[1:2], -1), shift(beside[1:2], 1)), beside[1:2])

    def near_depth(row):
        return jnp.where(lon_odd, row[:, 1:2], row[:, 0:1])

    def far_depth(row):
        return jnp.where(lon_odd, row[:, 0:1], row[:, 127:128])

    def by_side(even_part, odd_part):
        return jnp.where(lat_odd, even_part, odd_part), jnp.where(lat_odd, odd_part, even_part)

    def west_east(near_part, far_part):
        return jnp.where(lon_odd, near_part, far_part), jnp.where(lon_odd, far_part, near_part)

    near_s, near_n = by_side(near_even, near_odd)
    far_s, far_n = by_side(far_even, far_odd)
    (sw, se), (nw, ne) = west_east(near_s, far_s), west_east(near_n, far_n)
    near_sd, near_nd = by_side(near_depth(near_even_d), near_depth(near_odd_d))
    far_sd, far_nd = by_side(far_depth(far_cols[42:43]), far_depth(far_odd_d))
    corner_depth = [west_east(near_sd, far_sd), west_east(near_nd, far_nd)]
    odd_west = jnp.where(at_top, swap_pair(odd_info[1:2]), odd_info[0:1])
    odd_east = jnp.where(at_top, swap_pair(odd_info[0:1]), odd_info[1:2])
    own_sw, own_nw = by_side(even_rows[130:131], odd_west)
    own_se, own_ne = by_side(even_rows[131:132], odd_east)

    cols, col_depth = column_groups(packed, depth, west_cols, east_cols)
    cols_s, cols_n, corner_rows = [], [], []
    for out, w, e, own_w, own_e in ((cols_s, sw, se, own_sw, own_se), (cols_n, nw, ne, own_nw, own_ne)):
        for f in range(4):
            x = jnp.where(place1 == 5, shift(w, 4 - 2 * f), shift(e, 2 - 2 * f))
            x = jnp.where(place1 == 6, shift(own_w, 6 - 2 * f), x)
            out.append(jnp.where(place1 == 1, shift(own_e, -2 * f), x))
    for (w, e), own in zip(corner_depth, (south_rows[128:129], north_rows[128:129])):
        x = jnp.where(place1 == 5, w, e)
        x = jnp.where(place1 == 6, own[:, 0:1], x)
        corner_rows.append(jnp.where(place1 == 1, own[:, 127:128], x))

    wets = [
        as_wet(level < x)
        for x in (
            shift(col_depth, -1),
            shift(col_depth, 1),
            north_of(col_depth, corner_rows[1]),
            south_of(col_depth, corner_rows[0]),
        )
    ]
    cols_mid = five_point(
        cols,
        [shift(x, -1) for x in cols],
        [shift(x, 1) for x in cols],
        [north_of(x, y) for x, y in zip(cols, cols_n)],
        [south_of(x, y) for x, y in zip(cols, cols_s)],
        [shift(x, -8) for x in cols[:2]],
        [shift(x, 8) for x in cols[:2]],
        as_wet(level < col_depth),
        wets,
        as_wet(level + 1.0 < col_depth),
        as_wet(jnp.logical_and(lane >= 8, level - 1.0 < col_depth)),
        cosine,
        sine,
    )

    lane16 = lanes_of((LEVELS, LANES))
    sub16 = lax.broadcasted_iota(jnp.int32, (LEVELS, LANES), 0)
    lev16 = sub16.astype(jnp.float32)

    def one_row(c, n, s, ends, ends_d, d0, d_n, d_s, cos_row, sin_row):
        d_w = jnp.where(lane1 == 0, ends_d[0], shift(d0, 1))
        d_e = jnp.where(lane1 == 127, ends_d[1], shift(d0, -1))
        e, w = [], []
        for f in range(4):
            spread_out = jnp.broadcast_to(ends[f], (LEVELS, LANES))
            at_w = jnp.sum(jnp.where(lane16 == 8 * sub16 + 5, spread_out, 0.0), axis=1, keepdims=True)
            at_e = jnp.sum(jnp.where(lane16 == 8 * sub16 + 2, spread_out, 0.0), axis=1, keepdims=True)
            w.append(jnp.where(lane16 == 0, at_w, shift(c[f], 1)))
            e.append(jnp.where(lane16 == 127, at_e, shift(c[f], -1)))
        return five_point(
            c, e, w, n, s,
            [north_of(x, x[15:16]) for x in c[:2]],
            [south_of(x, x[0:1]) for x in c[:2]],
            as_wet(lev16 < d0),
            [as_wet(lev16 < x) for x in (d_e, d_w, d_n, d_s)],
            as_wet(lev16 + 1.0 < d0),
            as_wet(jnp.logical_and(sub16 >= 1, lev16 - 1.0 < d0)),
            cos_row,
            sin_row,
        )

    def of_rows(rows, d):
        at = 64 * d
        return [rows[at + f * 16 : at + f * 16 + 16] for f in range(4)]

    bottom = [x[:, 0, :] for x in fields]
    top = [x[:, ROWS - 1, :] for x in fields]
    south_mid = one_row(
        of_rows(south_rows, 0), bottom, of_rows(south_rows, 1), cols_s, corner_depth[0],
        south_rows[128:129], depth[0:1], south_rows[129:130], angles[64:65, :], angles[66:67, :],
    )
    north_mid = one_row(
        of_rows(north_rows, 0), of_rows(north_rows, 1), top, cols_n, corner_depth[1],
        north_rows[128:129], north_rows[129:130], depth[31:32], angles[65:66, :], angles[67:68, :],
    )

    def outer(top_part, bottom_part):
        return jnp.where(lat_odd, top_part, bottom_part)

    inner = [outer(x[:, ROWS - 2, :], x[:, 1, :]) for x in fields]
    beyond = of_rows(odd_rows, 0)
    inner_d, beyond_d = outer(depth[30:31], depth[1:2]), odd_rows[128:129]
    ends_d = outer(col_depth[31:32], col_depth[0:1])
    outer_mid = one_row(
        [outer(x, y) for x, y in zip(top, bottom)],
        [outer(x, y) for x, y in zip(beyond, inner)],
        [outer(x, y) for x, y in zip(inner, beyond)],
        [outer(x[31:32], x[0:1]) for x in cols],
        (ends_d[:, 5:6], ends_d[:, 2:3]),
        outer(depth[31:32], depth[0:1]),
        outer(beyond_d, inner_d),
        outer(inner_d, beyond_d),
        outer(cosine[31:32], cosine[0:1]),
        outer(sine[31:32], sine[0:1]),
    )

    row = lax.broadcasted_iota(jnp.int32, (ROWS, LANES), 0)
    redone_row = row == outer(ROWS - 1, 0)
    rim = jnp.logical_or(lane == 0, lane == 127)
    rims = [jnp.where(place == 1, x, shift(x, -4)) for x in cols_mid]

    def patched(f, k):
        x = jnp.where(rim, shift(rims[f], 127 - (8 * k + 1)), mid[f, k])
        return jnp.where(redone_row, outer_mid[f][k : k + 1], x)

    outs = (heat_out, salt_out, zonal_out, merid_out)
    copies = []

    def to_out(f, k, value):
        last[f, k] = value
        if k % CHUNK == CHUNK - 1:
            part = pl.ds(k + 1 - CHUNK, CHUNK)
            copy = pltpu.make_async_copy(last.at[f, part], outs[f].at[part], sems.at[f, k // CHUNK])
            copy.start()
            copies.append(copy)

    whole_step(
        patched,
        cols_mid,
        south_mid,
        north_mid,
        to_out,
        depth,
        depths_beside(depth, col_depth, south_rows[128:129], north_rows[128:129]),
        cosine,
        sine,
    )
    for copy in copies:
        copy.wait()


def shapes(*dims):
    return [jax.ShapeDtypeStruct(d, jnp.float32) for d in dims]


def call(kernel, outputs, *operands, scratch=(), held_in=True, held_out=True, grant=32, cost=False):
    vmem, hbm = pl.BlockSpec(memory_space=pltpu.VMEM), pl.BlockSpec(memory_space=pltpu.HBM)
    return pl.pallas_call(
        kernel,
        out_shape=shapes(*outputs),
        in_specs=[vmem if held_in else hbm] * len(operands),
        out_specs=[vmem if held_out else hbm] * len(outputs),
        scratch_shapes=list(scratch),
        cost_estimate=pl.CostEstimate(flops=30_000_000, bytes_accessed=2 << 20, transcendentals=0) if cost else None,
        compiler_params=pltpu.CompilerParams(vmem_limit_bytes=int(grant * 1024 * 1024)),
    )(*operands)


def angle_table():
    first = lax.axis_index("lat") * ROWS
    total = ROWS * N_LAT
    ids = jnp.concatenate([jnp.arange(ROWS), jnp.array([-1, ROWS])]) + first
    ids = jnp.where(ids >= total, 2 * total - 1 - ids, ids)
    angle = ROTATION * (2.0 * (ids.astype(jnp.float32) + 0.5) / total - 1.0)
    c, s = jnp.cos(angle), jnp.sin(angle)
    column = jnp.concatenate([c[:ROWS], s[:ROWS], c[ROWS:], s[ROWS:], jnp.zeros((4,), jnp.float32)])
    return jnp.broadcast_to(column[:, None], (72, LANES))


def on_device(heat, salt, zonal, merid, flag, tally):
    whole = (heat, salt, zonal, merid, flag, tally)
    size = (LEVELS, ROWS, LANES)
    pinned = [pltpu.with_memory_space_constraint(x, pltpu.HBM) for x in whole]
    *fields, depth, packed, info_top, info_bottom, col_near, col_far = call(
        pack_kernel,
        [size] * 4 + [(ROWS, LANES), (4, ROWS, LANES), (8, LANES), (8, LANES), (40, LANES), (40, LANES)],
        *pinned,
        scratch=[pltpu.VMEM((ROWS, LANES), jnp.int32)] * 2 + [pltpu.SemaphoreType.DMA((6,))],
        held_in=False,
    )
    near = send(col_near, near_lon, lambda lat, lon: True)
    rows = call(row_kernel, [(128, LANES)] * 3, *fields)
    row_low, row_odd, row_up = call(join_kernel, [(ROW_MSG, LANES)] * 3, *rows, info_top, info_bottom, near)
    even_low = send(row_low, even_lat, lambda lat, lon: not upper(lon))
    odd = send(row_odd, odd_or_diagonal, lambda lat, lon: lat > 0)
    even_up = send(row_up, even_lat, lambda lat, lon: upper(lon))
    to_far, to_far_edge = call(
        relay_kernel, [(COL_MSG, LANES), (EDGE_MSG, LANES)], even_low, odd, even_up, col_far
    )
    far = send(to_far, far_lon, lambda lat, lon: not is_edge(lat))
    far_edge = send(to_far_edge, far_lon, lambda lat, lon: is_edge(lat))
    known = (*fields, depth, packed, angle_table(), even_low, odd, even_up, near)
    (mid,) = call(early_kernel, [(4,) + size], *known, cost=True)
    return tuple(
        call(
            step_kernel,
            [size] * 4,
            mid, *known, far_edge, far,
            scratch=[
                pltpu.VMEM((ROW_MSG, LANES), jnp.float32),
                pltpu.VMEM((4,) + size, jnp.float32),
                pltpu.SemaphoreType.DMA((4, LEVELS // CHUNK)),
            ],
            held_out=False,
        )
    )


def solution(mesh):
    field, column = P(None, "lat", "lon"), P("lat", "lon")
    return jax.shard_map(
        on_device,
        mesh=mesh,
        in_specs=(field,) * 4 + (column,) * 2,
        out_specs=(field,) * 4,
        check_vma=False,
    )
```

time: 45 us -> 43.5 us (0.967)
  waiting for transfers between devices: 7.48 us -> 5.71 us
  Pallas kernels: 6.43 us -> 6.9 us
    ppermute x6, waiting for transfers between devices: 7.48 us -> 5.71 us  [send(): return lax.ppermute(array, ('lat', 'lon'), pairs(where_to, member))]
    pallas_call x4 -> x6, Pallas kernels: 6.43 us -> 6.9 us  [call(): pl.pallas_call(kernel, out_shape=shapes(*outputs), in_specs=[vmem if held...]
  transfers between devices with their start and end apart: 6 -> 6, of which waited for: 3 -> 3; matrix products, arithmetic and copies ran while one was open for 1% -> 1% of each run, Pallas kernels for 0% -> 4%
where the time goes in v3:
time: 43.5 us; the launch traced here: 43.2 us
  starting transfers between devices  29.4 us (68%)
  Pallas kernels  6.9 us (16%)
  waiting for transfers between devices  5.71 us (13%)
  between operations  0.76 us (2%)
    ppermute x6, starting transfers between devices, send(): return lax.ppermute(array, ('lat', 'lon'), pairs(where_to, member))  29.4 us
    pallas_call x6, Pallas kernels, call(): pl.pallas_call(kernel, out_shape=shapes(*outputs), in_specs=[vmem if held...  6.9 us
    ppermute x6, waiting for transfers between devices, send(): return lax.ppermute(array, ('lat', 'lon'), pairs(where_to, member))  5.71 us
  transfers between devices with their start and end apart: 6, of which 3 were waited for; matrix products, arithmetic and copies ran while one was open for 1% of the time, Pallas kernels for 4%

profile of v3, /device:TPU:6, one launch (start us, length us, event | category | flops | bytes accessed | tf_op | source)
XLA Modules:
  0.0 43.2 jit_solution(4223132497754579283)
XLA Ops:
  0.6 1.9 %shard_map.102 = (f32[16,32,128]{2,1,0:T(8,128)S(1)}, f32[16,32,128]{2,1,0:T(8,128)S(1)}, f32[16,32,128]{2,1,0:T(8,128)S(1)}, f32[16,32,128]{2,1,0:T(8,128)S(1)}...) custom-call(f32[16,32,128]{2,1,0:T(8,128)} %heat_in.1, ...), custom_call_target="tpu_custom_call" | custom-call | tf_op jit(solution)/shard_map/pallas_call | solution.py:562
  2.5 1.9 %collective-permute-start = (f32[40,128]{1,0:T(8,128)S(1)}, f32[40,128]{1,0:T(8,128)S(1)}, u32[]{:S(2)}, u32[]{:S(2)}) collective-permute-start(f32[40,128]{1,0:T(8,128)S(1)} %get-tuple-element.33), channel_id=1, source_target_pairs={{0,1},{1,0},{2,3},{3,2},{4,5},{5,4},{6,7},{7,6},{8,9},{9,8},{10,11... | collective-permute-start | bytes 61448 | tf_op jit(solution)/shard_map/ppermute | solution.py:60
  4.4 0.1 shard_map.103
  4.5 1.0 %collective-permute-done.near = f32[40,128]{1,0:T(8,128)S(1)} collective-permute-done((f32[40,128]{1,0:T(8,128)S(1)}, f32[40,128]{1,0:T(8,128)S(1)}, u32[]{:S(2)}, u32[]{:S(2)}) %collective-permute-start) | collective-permute-done | bytes 20512 | tf_op jit(solution)/shard_map/ppermute | solution.py:60
  5.6 0.1 shard_map.104
  5.7 3.8 %collective-permute-start.1 = (f32[136,128]{1,0:T(8,128)S(1)}, f32[136,128]{1,0:T(8,128)S(1)}, u32[]{:S(2)}, u32[]{:S(2)}) collective-permute-start(f32[136,128]{1,0:T(8,128)S(1)} %get-tuple-element.34), channel_id=1, source_target_pairs={{0,16},{1,17},{4,20},{5,21},{8,24},{9,25},{12,28},{13,29},{16,0},{... | collective-permute-start | bytes 208904 | tf_op jit(solution)/shard_map/ppermute | solution.py:60
  9.5 10.7 %collective-permute-start.2 = (f32[136,128]{1,0:T(8,128)S(1)}, f32[136,128]{1,0:T(8,128)S(1)}, u32[]{:S(2)}, u32[]{:S(2)}) collective-permute-start(f32[136,128]{1,0:T(8,128)S(1)} %get-tuple-element.35), channel_id=1, source_target_pairs={{16,32},{17,33},{18,34},{19,35},{20,36},{21,37},{22,38},{23,39},{2... | collective-permute-start | bytes 208904 | tf_op jit(solution)/shard_map/ppermute | solution.py:60
  20.2 0.7 %collective-permute-start.3 = (f32[136,128]{1,0:T(8,128)S(1)}, f32[136,128]{1,0:T(8,128)S(1)}, u32[]{:S(2)}, u32[]{:S(2)}) collective-permute-start(f32[136,128]{1,0:T(8,128)S(1)} %get-tuple-element.36), channel_id=1, source_target_pairs={{2,18},{3,19},{6,22},{7,23},{10,26},{11,27},{14,30},{15,31},{18,2}... | collective-permute-start | bytes 208904 | tf_op jit(solution)/shard_map/ppermute | solution.py:60
  20.9 0.0 collective-permute-done.1.even_low
  20.9 1.6 %collective-permute-done.2.odd = f32[136,128]{1,0:T(8,128)S(1)} collective-permute-done((f32[136,128]{1,0:T(8,128)S(1)}, f32[136,128]{1,0:T(8,128)S(1)}, u32[]{:S(2)}, u32[]{:S(2)}) %collective-permute-start.2) | collective-permute-done | bytes 69664 | tf_op jit(solution)/shard_map/ppermute | solution.py:60
  22.5 0.0 collective-permute-done.3.even_up
  22.5 0.0 copy-start
  22.5 0.7 %collective-permute-start.5 = (f32[48,128]{1,0:T(8,128)S(1)}, f32[48,128]{1,0:T(8,128)S(1)}, u32[]{:S(2)}, u32[]{:S(2)}) collective-permute-start(f32[48,128]{1,0:T(8,128)S(1)} %get-tuple-element.39), channel_id=1, source_target_pairs={{0,15},{1,2},{2,1},{3,4},{4,3},{5,6},{6,5},{7,8},{8,7},{9,10},{10,... | collective-permute-start | bytes 73736 | tf_op jit(solution)/shard_map/ppermute | solution.py:60
  23.2 11.6 %collective-permute-start.4 = (f32[184,128]{1,0:T(8,128)S(1)}, f32[184,128]{1,0:T(8,128)S(1)}, u32[]{:S(2)}, u32[]{:S(2)}) collective-permute-start(f32[184,128]{1,0:T(8,128)S(1)} %get-tuple-element.38), channel_id=1, source_target_pairs={{112,127},{113,114},{114,113},{115,116},{116,115},{117,118},{118,1... | collective-permute-start | bytes 282632 | tf_op jit(solution)/shard_map/ppermute | solution.py:60
  34.8 0.0 copy-done
  34.9 0.1 slice.14
  35.0 0.1 slice.15
  35.1 0.1 concatenate.7
  35.2 0.1 broadcast_in_dim.2.angles
  35.2 1.6 %shard_map.105.mid = f32[4,16,32,128]{3,2,1,0:T(8,128)S(1)} custom-call(f32[16,32,128]{2,1,0:T(8,128)S(1)} %get-tuple-element.22.heat, f32[16,32,128]{2,1,0:T(8,128)S(1)} %get-tuple-element.23.salt, f32[16,32,128]{2,1,0:T(8,128)S(1)} %get-tuple-element.24.zonal, f32[16,32,128]{2,1,0:T(8,128)S(1)} %get-tuple-element.25.merid, ...), custom_call_target="tpu_custom_call" | custom-call | flops 30000000 | bytes 2097152 | tf_op jit(solution)/shard_map/pallas_call | solution.py:562
  36.8 0.0 collective-permute-done.5.far
  36.8 3.1 %collective-permute-done.4.far_edge = f32[184,128]{1,0:T(8,128)S(1)} collective-permute-done((f32[184,128]{1,0:T(8,128)S(1)}, f32[184,128]{1,0:T(8,128)S(1)}, u32[]{:S(2)}, u32[]{:S(2)}) %collective-permute-start.4) | collective-permute-done | bytes 94240 | tf_op jit(solution)/shard_map/ppermute | solution.py:60
  39.9 3.3 %shard_map.107 = (f32[16,32,128]{2,1,0:T(8,128)}, f32[16,32,128]{2,1,0:T(8,128)}, f32[16,32,128]{2,1,0:T(8,128)}, f32[16,32,128]{2,1,0:T(8,128)}) custom-call(f32[4,16,32,128]{3,2,1,0:T(8,128)S(1)} %shard_map.105.mid, f32[16,32,128]{2,1,0:T(8,128)S(1)} %get-tuple-element.22.heat, f32[16,32,128]{2,1,0:T(8,128)S(1)} %get-tuple-element.23.salt, ...), custom_call_target="tpu_custom_call" | custom-call | tf_op jit(solution)/shard_map/pallas_call | solution.py:562
  (4 shorter events, 0.1 us)
Async XLA Ops:
  2.5 3.1 %collective-permute-start = (f32[40,128]{1,0:T(8,128)S(1)}, f32[40,128]{1,0:T(8,128)S(1)}, u32[]{:S(2)}, u32[]{:S(2)}) collective-permute-start(f32[40,128]{1,0:T(8,128)S(1)} %get-tuple-element.33), channel_id=1, source_target_pairs={{0,1},{1,0},{2,3},{3,2},{4,5},{5,4},{6,7},{7,6},{8,9},{9,8},{10,11... | collective-permute-start | bytes 61448 | tf_op jit(solution)/shard_map/ppermute | solution.py:60
  5.7 15.2 %collective-permute-start.1 = (f32[136,128]{1,0:T(8,128)S(1)}, f32[136,128]{1,0:T(8,128)S(1)}, u32[]{:S(2)}, u32[]{:S(2)}) collective-permute-start(f32[136,128]{1,0:T(8,128)S(1)} %get-tuple-element.34), channel_id=1, source_target_pairs={{0,16},{1,17},{4,20},{5,21},{8,24},{9,25},{12,28},{13,29},{16,0},{... | collective-permute-start | bytes 208904 | tf_op jit(solution)/shard_map/ppermute | solution.py:60
  9.5 13.0 %collective-permute-start.2 = (f32[136,128]{1,0:T(8,128)S(1)}, f32[136,128]{1,0:T(8,128)S(1)}, u32[]{:S(2)}, u32[]{:S(2)}) collective-permute-start(f32[136,128]{1,0:T(8,128)S(1)} %get-tuple-element.35), channel_id=1, source_target_pairs={{16,32},{17,33},{18,34},{19,35},{20,36},{21,37},{22,38},{23,39},{2... | collective-permute-start | bytes 208904 | tf_op jit(solution)/shard_map/ppermute | solution.py:60
  20.2 2.3 %collective-permute-start.3 = (f32[136,128]{1,0:T(8,128)S(1)}, f32[136,128]{1,0:T(8,128)S(1)}, u32[]{:S(2)}, u32[]{:S(2)}) collective-permute-start(f32[136,128]{1,0:T(8,128)S(1)} %get-tuple-element.36), channel_id=1, source_target_pairs={{2,18},{3,19},{6,22},{7,23},{10,26},{11,27},{14,30},{15,31},{18,2}... | collective-permute-start | bytes 208904 | tf_op jit(solution)/shard_map/ppermute | solution.py:60
  22.5 12.3 %copy-start = (s32[34]{0:T(128)S(1)}, s32[34]{0:T(128)}, u32[]{:S(2)}) copy-start(s32[34]{0:T(128)} %constant.29) | copy-start | bytes 412
  22.5 14.3 %collective-permute-start.5 = (f32[48,128]{1,0:T(8,128)S(1)}, f32[48,128]{1,0:T(8,128)S(1)}, u32[]{:S(2)}, u32[]{:S(2)}) collective-permute-start(f32[48,128]{1,0:T(8,128)S(1)} %get-tuple-element.39), channel_id=1, source_target_pairs={{0,15},{1,2},{2,1},{3,4},{4,3},{5,6},{6,5},{7,8},{8,7},{9,10},{10,... | collective-permute-start | bytes 73736 | tf_op jit(solution)/shard_map/ppermute | solution.py:60
  23.2 16.7 %collective-permute-start.4 = (f32[184,128]{1,0:T(8,128)S(1)}, f32[184,128]{1,0:T(8,128)S(1)}, u32[]{:S(2)}, u32[]{:S(2)}) collective-permute-start(f32[184,128]{1,0:T(8,128)S(1)} %get-tuple-element.38), channel_id=1, source_target_pairs={{112,127},{113,114},{114,113},{115,116},{116,115},{117,118},{118,1... | collective-permute-start | bytes 282632 | tf_op jit(solution)/shard_map/ppermute | solution.py:60

commit v4 on v3

--- a/solution.py
+++ b/solution.py
@@ -17,6 +17,7 @@
 ROW_MSG = 136
 COL_MSG = 48
 CHUNK = 4
+FETCHES = 1
 EDGE_MSG = COL_MSG + ROW_MSG
 
 
@@ -78,6 +79,11 @@
     return lax.axis_index("lat"), lax.axis_index("lon")
 
 
+def is_edge_run(lat):
+    run = lax.rem(lat, BLOCK)
+    return jnp.logical_and(lat > 0, jnp.logical_or(run == 0, run == BLOCK - 1))
+
+
 def is_upper(lon):
     return lax.rem(lax.div(lon, 2), 2) == 1
 
@@ -87,15 +93,12 @@
     heat, salt, zonal, merid, depth_out, packed, info_top, info_bottom, col_near, col_far,
     flag, tally, sems,
 ):
-    copies = [
-        pltpu.make_async_copy(source, held, sems.at[i])
-        for i, (source, held) in enumerate(
-            (
-                (flag_in, flag), (tally_in, tally), (heat_in, heat),
-                (salt_in, salt), (zonal_in, zonal), (merid_in, merid),
-            )
-        )
-    ]
+    sources, fields = (heat_in, salt_in, zonal_in, merid_in), (heat, salt, zonal, merid)
+    copies = [pltpu.make_async_copy(*x, sems.at[i]) for i, x in enumerate(((flag_in, flag), (tally_in, tally)))]
+    for i in range(4 * FETCHES):
+        part = pl.ds(i % FETCHES * (LEVELS // FETCHES), LEVELS // FETCHES)
+        f = i // FETCHES
+        copies.append(pltpu.make_async_copy(sources[f].at[part], fields[f].at[part], sems.at[2 + i]))
     for copy in copies:
         copy.start()
     _, lon = position()
@@ -109,10 +112,11 @@
     pair = (lane & 7) >> 1
     west = jnp.zeros((ROWS, LANES), jnp.float32)
     east = west
-    for f, field in enumerate((heat, salt, zonal, merid)):
-        copies[2 + f].wait()
+    for f, field in enumerate(fields):
         acc = jnp.zeros((ROWS, LANES), jnp.float32)
         for k in range(LEVELS):
+            if k % (LEVELS // FETCHES) == 0:
+                copies[2 + f * FETCHES + k // (LEVELS // FETCHES)].wait()
             acc = jnp.where(group == k, shift(field[k], 8 * k + 2), acc)
         packed[f] = acc
         west = jnp.where(pair == f, shift(acc, 2 * f - 2), west)
@@ -180,6 +184,23 @@
     to_far_edge[0:40, :] = col_far[...]
     to_far_edge[40:48, :] = far_tile
     to_far_edge[48:184, :] = odd[...]
+
+
+def near_kernel(even_low, odd, even_up, far_edge, col_near, _, to_near):
+    lat, lon = position()
+    lon_odd = lax.rem(lon, 2) == 1
+    at_top = lat == N_LAT - 1
+    even_info = jnp.where(is_upper(lon), even_up[128:136, :], even_low[128:136, :])
+    odd_info = jnp.where(is_edge_run(lat), far_edge[176:184, :], odd[128:136, :])
+
+    def beside(info, first):
+        return jnp.where(first, info[2:3], info[3:4]), jnp.where(first, info[0:1], shift(info[0:1], 2))
+
+    to_near[0:40, :] = col_near[...]
+    blank = jnp.zeros((4, LANES), jnp.float32)
+    to_near[40:48, :] = jnp.concatenate(
+        [*beside(even_info, lon_odd), *beside(odd_info, jnp.logical_xor(lon_odd, at_top)), blank], 0
+    )
 
 
 def reversed_lanes(x):
@@ -343,15 +364,15 @@
 
 
 def step_kernel(
-    mid, heat, salt, zonal, merid, depth_in, packed, angles, even_low, odd, even_up, near, far_edge, far,
+    mid, heat, salt, zonal, merid, depth_in, packed, angles, even_low, odd, even_up, near, near_up, far_edge, far,
     heat_out, salt_out, zonal_out, merid_out, turned, last, sems,
 ):
     lat, lon = position()
     lat_odd = lax.rem(lat, 2) == 1
     lon_odd = lax.rem(lon, 2) == 1
     at_top = lat == N_LAT - 1
-    run = lax.rem(lat, BLOCK)
-    edge = jnp.logical_and(lat > 0, jnp.logical_or(run == 0, run == BLOCK - 1))
+    edge = is_edge_run(lat)
+    late = is_upper(lon)
     fields = (heat, salt, zonal, merid)
     lane = lanes_of((ROWS, LANES))
     place = lane & 7
@@ -376,13 +397,15 @@
             part = reversed_lanes(odd_rows[at : min(at + 16, 130)])
             turned[at : min(at + 16, 130), :] = -part if at < 128 and at // 16 % 4 >= 2 else part
 
+    even_rows = jnp.where(is_upper(lon), even_up[...], even_low[...])
+    even_beside = jnp.where(late, near_up[40:42, :], even_rows[132:134])
+    beside = jnp.where(late, near_up[42:44, :], beside)
     odd_info = odd_rows[130:132]
     odd_rows = turned[...]
-    even_rows = jnp.where(is_upper(lon), even_up[...], even_low[...])
     south_rows = jnp.where(lat_odd, even_rows, odd_rows)
     north_rows = jnp.where(lat_odd, odd_rows, even_rows)
     far_cols = jnp.where(edge, far_edge[0:48, :], far[...])
-    near_cols = near[...]
+    near_cols = jnp.where(late, near_up[0:40, :], near[...])
     west_cols = jnp.where(lon_odd, near_cols, far_cols[0:40])
     east_cols = jnp.where(lon_odd, far_cols[0:40], near_cols)
 
@@ -393,7 +416,7 @@
     far_even = far_cols[40:41]
     far_odd = jnp.where(edge, jnp.where(lon_odd, q_west, q_east), far_cols[41:42])
     far_odd_d = jnp.where(edge, q_depth, far_cols[43:44])
-    near_even, near_even_d = even_rows[132:133], even_rows[133:134]
+    near_even, near_even_d = even_beside[0:1], even_beside[1:2]
     near_odd = jnp.where(at_top, swap_pair(beside[0:1]), beside[0:1])
     near_odd_d = jnp.where(at_top, jnp.where(lane1 == 0, shift(beside[1:2], -1), shift(beside[1:2], 1)), beside[1:2])
 
@@ -589,10 +612,10 @@
         pack_kernel,
         [size] * 4 + [(ROWS, LANES), (4, ROWS, LANES), (8, LANES), (8, LANES), (40, LANES), (40, LANES)],
         *pinned,
-        scratch=[pltpu.VMEM((ROWS, LANES), jnp.int32)] * 2 + [pltpu.SemaphoreType.DMA((6,))],
+        scratch=[pltpu.VMEM((ROWS, LANES), jnp.int32)] * 2 + [pltpu.SemaphoreType.DMA((2 + 4 * FETCHES,))],
         held_in=False,
     )
-    near = send(col_near, near_lon, lambda lat, lon: True)
+    near = send(col_near, near_lon, lambda lat, lon: not upper(lon) or lat == N_LAT - 1)
     rows = call(row_kernel, [(128, LANES)] * 3, *fields)
     row_low, row_odd, row_up = call(join_kernel, [(ROW_MSG, LANES)] * 3, *rows, info_top, info_bottom, near)
     even_low = send(row_low, even_lat, lambda lat, lon: not upper(lon))
@@ -605,11 +628,13 @@
     far_edge = send(to_far_edge, far_lon, lambda lat, lon: is_edge(lat))
     known = (*fields, depth, packed, angle_table(), even_low, odd, even_up, near)
     (mid,) = call(early_kernel, [(4,) + size], *known, cost=True)
+    (to_near,) = call(near_kernel, [(COL_MSG, LANES)], even_low, odd, even_up, far_edge, col_near, mid)
+    near_up = send(to_near, near_lon, lambda lat, lon: upper(lon))
     return tuple(
         call(
             step_kernel,
             [size] * 4,
-            mid, *known, far_edge, far,
+            mid, *known, near_up, far_edge, far,
             scratch=[
                 pltpu.VMEM((ROW_MSG, LANES), jnp.float32),
                 pltpu.VMEM((4,) + size, jnp.float32),

time: 43.5 us -> 41.6 us (0.956)
  waiting for transfers between devices: 5.71 us -> 4.37 us
  starting transfers between devices: 29.4 us -> 28.8 us
    ppermute x6 -> x7, waiting for transfers between devices: 5.71 us -> 4.37 us  [send(): return lax.ppermute(array, ('lat', 'lon'), pairs(where_to, member))]
    ppermute x6 -> x7, starting transfers between devices: 29.4 us -> 28.8 us  [send(): return lax.ppermute(array, ('lat', 'lon'), pairs(where_to, member))]
    pallas_call x6 -> x7, Pallas kernels: 6.9 us -> 6.95 us  [call(): pl.pallas_call(kernel, out_shape=shapes(*outputs), in_specs=[vmem if held...]
  transfers between devices with their start and end apart: 6 -> 7, of which waited for: 3 -> 3; matrix products, arithmetic and copies ran while one was open for 1% -> 1% of each run, Pallas kernels for 4% -> 4%
where the time goes in v4:
time: 41.6 us; the launch traced here: 41.3 us
  starting transfers between devices  28.8 us (69%)
  Pallas kernels  6.95 us (17%)
  waiting for transfers between devices  4.37 us (11%)
  between operations  0.77 us (2%)
    ppermute x7, starting transfers between devices, send(): return lax.ppermute(array, ('lat', 'lon'), pairs(where_to, member))  28.8 us
    pallas_call x7, Pallas kernels, call(): pl.pallas_call(kernel, out_shape=shapes(*outputs), in_specs=[vmem if held...  6.95 us
    ppermute x7, waiting for transfers between devices, send(): return lax.ppermute(array, ('lat', 'lon'), pairs(where_to, member))  4.37 us
  transfers between devices with their start and end apart: 7, of which 3 were waited for; matrix products, arithmetic and copies ran while one was open for 1% of the time, Pallas kernels for 4%

profile of v4, /device:TPU:6, one launch (start us, length us, event | category | flops | bytes accessed | tf_op | source)
XLA Modules:
  0.0 41.3 jit_solution(15130959833424501343)
XLA Ops:
  0.6 1.9 %shard_map.102 = (f32[16,32,128]{2,1,0:T(8,128)S(1)}, f32[16,32,128]{2,1,0:T(8,128)S(1)}, f32[16,32,128]{2,1,0:T(8,128)S(1)}, f32[16,32,128]{2,1,0:T(8,128)S(1)}...) custom-call(f32[16,32,128]{2,1,0:T(8,128)} %heat_in.1, ...), custom_call_target="tpu_custom_call" | custom-call | tf_op jit(solution)/shard_map/pallas_call | solution.py:585
  2.5 1.9 %collective-permute-start = (f32[40,128]{1,0:T(8,128)S(1)}, f32[40,128]{1,0:T(8,128)S(1)}, u32[]{:S(2)}, u32[]{:S(2)}) collective-permute-start(f32[40,128]{1,0:T(8,128)S(1)} %get-tuple-element.33.col_near), channel_id=1, source_target_pairs={{0,1},{1,0},{4,5},{5,4},{8,9},{9,8},{12,13},{13,12},{16,17},{17,16... | collective-permute-start | bytes 61448 | tf_op jit(solution)/shard_map/ppermute | solution.py:61
  4.4 0.1 shard_map.103
  4.5 1.0 %collective-permute-done.near = f32[40,128]{1,0:T(8,128)S(1)} collective-permute-done((f32[40,128]{1,0:T(8,128)S(1)}, f32[40,128]{1,0:T(8,128)S(1)}, u32[]{:S(2)}, u32[]{:S(2)}) %collective-permute-start) | collective-permute-done | bytes 20512 | tf_op jit(solution)/shard_map/ppermute | solution.py:61
  5.6 0.1 shard_map.104
  5.7 3.8 %collective-permute-start.1 = (f32[136,128]{1,0:T(8,128)S(1)}, f32[136,128]{1,0:T(8,128)S(1)}, u32[]{:S(2)}, u32[]{:S(2)}) collective-permute-start(f32[136,128]{1,0:T(8,128)S(1)} %get-tuple-element.34), channel_id=1, source_target_pairs={{0,16},{1,17},{4,20},{5,21},{8,24},{9,25},{12,28},{13,29},{16,0},{... | collective-permute-start | bytes 208904 | tf_op jit(solution)/shard_map/ppermute | solution.py:61
  9.5 8.1 %collective-permute-start.2 = (f32[136,128]{1,0:T(8,128)S(1)}, f32[136,128]{1,0:T(8,128)S(1)}, u32[]{:S(2)}, u32[]{:S(2)}) collective-permute-start(f32[136,128]{1,0:T(8,128)S(1)} %get-tuple-element.35), channel_id=1, source_target_pairs={{16,32},{17,33},{18,34},{19,35},{20,36},{21,37},{22,38},{23,39},{2... | collective-permute-start | bytes 208904 | tf_op jit(solution)/shard_map/ppermute | solution.py:61
  17.6 0.7 %collective-permute-start.3 = (f32[136,128]{1,0:T(8,128)S(1)}, f32[136,128]{1,0:T(8,128)S(1)}, u32[]{:S(2)}, u32[]{:S(2)}) collective-permute-start(f32[136,128]{1,0:T(8,128)S(1)} %get-tuple-element.36), channel_id=1, source_target_pairs={{2,18},{3,19},{6,22},{7,23},{10,26},{11,27},{14,30},{15,31},{18,2}... | collective-permute-start | bytes 208904 | tf_op jit(solution)/shard_map/ppermute | solution.py:61
  18.3 0.0 collective-permute-done.1.even_low
  18.3 1.3 %collective-permute-done.2.odd = f32[136,128]{1,0:T(8,128)S(1)} collective-permute-done((f32[136,128]{1,0:T(8,128)S(1)}, f32[136,128]{1,0:T(8,128)S(1)}, u32[]{:S(2)}, u32[]{:S(2)}) %collective-permute-start.2) | collective-permute-done | bytes 69664 | tf_op jit(solution)/shard_map/ppermute | solution.py:61
  19.6 0.0 collective-permute-done.3.even_up
  19.6 0.0 copy-start
  19.6 13.0 %collective-permute-start.4 = (f32[184,128]{1,0:T(8,128)S(1)}, f32[184,128]{1,0:T(8,128)S(1)}, u32[]{:S(2)}, u32[]{:S(2)}) collective-permute-start(f32[184,128]{1,0:T(8,128)S(1)} %get-tuple-element.38), channel_id=1, source_target_pairs={{112,127},{113,114},{114,113},{115,116},{116,115},{117,118},{118,1... | collective-permute-start | bytes 282632 | tf_op jit(solution)/shard_map/ppermute | solution.py:61
  32.6 0.0 copy-done
  32.7 0.1 slice.14
  32.8 0.1 slice.15
  32.9 0.1 concatenate.7
  32.9 0.7 %collective-permute-start.6 = (f32[48,128]{1,0:T(8,128)S(1)}, f32[48,128]{1,0:T(8,128)S(1)}, u32[]{:S(2)}, u32[]{:S(2)}) collective-permute-start(f32[48,128]{1,0:T(8,128)S(1)} %get-tuple-element.39), channel_id=1, source_target_pairs={{0,15},{1,2},{2,1},{3,4},{4,3},{5,6},{6,5},{7,8},{8,7},{9,10},{10,... | collective-permute-start | bytes 73736 | tf_op jit(solution)/shard_map/ppermute | solution.py:61
  33.6 0.1 broadcast_in_dim.2.angles
  33.7 1.6 %shard_map.105._.mid = f32[4,16,32,128]{3,2,1,0:T(8,128)S(1)} custom-call(f32[16,32,128]{2,1,0:T(8,128)S(1)} %get-tuple-element.22.heat, f32[16,32,128]{2,1,0:T(8,128)S(1)} %get-tuple-element.23.salt, f32[16,32,128]{2,1,0:T(8,128)S(1)} %get-tuple-element.24.zonal, f32[16,32,128]{2,1,0:T(8,128)S(1)} %get-tuple-element.25.merid, ...), custom_call_target="tpu_custom_call" | custom-call | flops 30000000 | bytes 2097152 | tf_op jit(solution)/shard_map/pallas_call | solution.py:585
  35.2 2.0 %collective-permute-done.4.far_edge = f32[184,128]{1,0:T(8,128)S(1)} collective-permute-done((f32[184,128]{1,0:T(8,128)S(1)}, f32[184,128]{1,0:T(8,128)S(1)}, u32[]{:S(2)}, u32[]{:S(2)}) %collective-permute-start.4) | collective-permute-done | bytes 94240 | tf_op jit(solution)/shard_map/ppermute | solution.py:61
  37.3 0.1 shard_map.107
  37.4 0.7 %collective-permute-start.5 = (f32[48,128]{1,0:T(8,128)S(1)}, f32[48,128]{1,0:T(8,128)S(1)}, u32[]{:S(2)}, u32[]{:S(2)}) collective-permute-start(f32[48,128]{1,0:T(8,128)S(1)} %shard_map.107), channel_id=1, source_target_pairs={{2,3},{3,2},{6,7},{7,6},{10,11},{11,10},{14,15},{15,14},{18,19},{1... | collective-permute-start | bytes 73736 | tf_op jit(solution)/shard_map/ppermute | solution.py:61
  38.0 0.0 collective-permute-done.6.far
  38.0 0.0 collective-permute-done.5.near_up
  38.0 3.2 %shard_map.108 = (f32[16,32,128]{2,1,0:T(8,128)}, f32[16,32,128]{2,1,0:T(8,128)}, f32[16,32,128]{2,1,0:T(8,128)}, f32[16,32,128]{2,1,0:T(8,128)}) custom-call(f32[4,16,32,128]{3,2,1,0:T(8,128)S(1)} %shard_map.105._.mid, f32[16,32,128]{2,1,0:T(8,128)S(1)} %get-tuple-element.22.heat, f32[16,32,128]{2,1,0:T(8,128)S(1)} %get-tuple-element.23.salt, ...), custom_call_target="tpu_custom_call" | custom-call | tf_op jit(solution)/shard_map/pallas_call | solution.py:585
  (4 shorter events, 0.1 us)
Async XLA Ops:
  2.5 3.1 %collective-permute-start = (f32[40,128]{1,0:T(8,128)S(1)}, f32[40,128]{1,0:T(8,128)S(1)}, u32[]{:S(2)}, u32[]{:S(2)}) collective-permute-start(f32[40,128]{1,0:T(8,128)S(1)} %get-tuple-element.33.col_near), channel_id=1, source_target_pairs={{0,1},{1,0},{4,5},{5,4},{8,9},{9,8},{12,13},{13,12},{16,17},{17,16... | collective-permute-start | bytes 61448 | tf_op jit(solution)/shard_map/ppermute | solution.py:61
  5.7 12.6 %collective-permute-start.1 = (f32[136,128]{1,0:T(8,128)S(1)}, f32[136,128]{1,0:T(8,128)S(1)}, u32[]{:S(2)}, u32[]{:S(2)}) collective-permute-start(f32[136,128]{1,0:T(8,128)S(1)} %get-tuple-element.34), channel_id=1, source_target_pairs={{0,16},{1,17},{4,20},{5,21},{8,24},{9,25},{12,28},{13,29},{16,0},{... | collective-permute-start | bytes 208904 | tf_op jit(solution)/shard_map/ppermute | solution.py:61
  9.5 10.1 %collective-permute-start.2 = (f32[136,128]{1,0:T(8,128)S(1)}, f32[136,128]{1,0:T(8,128)S(1)}, u32[]{:S(2)}, u32[]{:S(2)}) collective-permute-start(f32[136,128]{1,0:T(8,128)S(1)} %get-tuple-element.35), channel_id=1, source_target_pairs={{16,32},{17,33},{18,34},{19,35},{20,36},{21,37},{22,38},{23,39},{2... | collective-permute-start | bytes 208904 | tf_op jit(solution)/shard_map/ppermute | solution.py:61
  17.6 2.0 %collective-permute-start.3 = (f32[136,128]{1,0:T(8,128)S(1)}, f32[136,128]{1,0:T(8,128)S(1)}, u32[]{:S(2)}, u32[]{:S(2)}) collective-permute-start(f32[136,128]{1,0:T(8,128)S(1)} %get-tuple-element.36), channel_id=1, source_target_pairs={{2,18},{3,19},{6,22},{7,23},{10,26},{11,27},{14,30},{15,31},{18,2}... | collective-permute-start | bytes 208904 | tf_op jit(solution)/shard_map/ppermute | solution.py:61
  19.6 13.0 %copy-start = (s32[34]{0:T(128)S(1)}, s32[34]{0:T(128)}, u32[]{:S(2)}) copy-start(s32[34]{0:T(128)} %constant.29) | copy-start | bytes 412
  19.6 17.7 %collective-permute-start.4 = (f32[184,128]{1,0:T(8,128)S(1)}, f32[184,128]{1,0:T(8,128)S(1)}, u32[]{:S(2)}, u32[]{:S(2)}) collective-permute-start(f32[184,128]{1,0:T(8,128)S(1)} %get-tuple-element.38), channel_id=1, source_target_pairs={{112,127},{113,114},{114,113},{115,116},{116,115},{117,118},{118,1... | collective-permute-start | bytes 282632 | tf_op jit(solution)/shard_map/ppermute | solution.py:61
  32.9 5.1 %collective-permute-start.6 = (f32[48,128]{1,0:T(8,128)S(1)}, f32[48,128]{1,0:T(8,128)S(1)}, u32[]{:S(2)}, u32[]{:S(2)}) collective-permute-start(f32[48,128]{1,0:T(8,128)S(1)} %get-tuple-element.39), channel_id=1, source_target_pairs={{0,15},{1,2},{2,1},{3,4},{4,3},{5,6},{6,5},{7,8},{8,7},{9,10},{10,... | collective-permute-start | bytes 73736 | tf_op jit(solution)/shard_map/ppermute | solution.py:61
  37.4 0.7 %collective-permute-start.5 = (f32[48,128]{1,0:T(8,128)S(1)}, f32[48,128]{1,0:T(8,128)S(1)}, u32[]{:S(2)}, u32[]{:S(2)}) collective-permute-start(f32[48,128]{1,0:T(8,128)S(1)} %shard_map.107), channel_id=1, source_target_pairs={{2,3},{3,2},{6,7},{7,6},{10,11},{11,10},{14,15},{15,14},{18,19},{1... | collective-permute-start | bytes 73736 | tf_op jit(solution)/shard_map/ppermute | solution.py:61

commit v5 on v4

--- a/solution.py
+++ b/solution.py
@@ -16,8 +16,7 @@
 BLOCK = 8
 ROW_MSG = 136
 COL_MSG = 48
-CHUNK = 4
-FETCHES = 1
+CHUNK = 8
 EDGE_MSG = COL_MSG + ROW_MSG
 
 
@@ -45,6 +44,10 @@
 
 def upper(lon):
     return lon // 2 % 2 == 1
+
+
+def meets_even_early(lat, lon):
+    return not upper(lon) and lat % BLOCK < BLOCK // 2
 
 
 def pairs(where_to, member):
@@ -88,39 +91,39 @@
     return lax.rem(lax.div(lon, 2), 2) == 1
 
 
+def is_late_even(lat, lon):
+    return jnp.logical_or(is_upper(lon), lax.rem(lat, BLOCK) >= BLOCK // 2)
+
+
 def pack_kernel(
     heat_in, salt_in, zonal_in, merid_in, flag_in, tally_in,
     heat, salt, zonal, merid, depth_out, packed, info_top, info_bottom, col_near, col_far,
     flag, tally, sems,
 ):
     sources, fields = (heat_in, salt_in, zonal_in, merid_in), (heat, salt, zonal, merid)
-    copies = [pltpu.make_async_copy(*x, sems.at[i]) for i, x in enumerate(((flag_in, flag), (tally_in, tally)))]
-    for i in range(4 * FETCHES):
-        part = pl.ds(i % FETCHES * (LEVELS // FETCHES), LEVELS // FETCHES)
-        f = i // FETCHES
-        copies.append(pltpu.make_async_copy(sources[f].at[part], fields[f].at[part], sems.at[2 + i]))
+    pairs_in = [*zip(sources, fields), (flag_in, flag), (tally_in, tally)]
+    copies = [pltpu.make_async_copy(*x, sems.at[i]) for i, x in enumerate(pairs_in)]
     for copy in copies:
         copy.start()
     _, lon = position()
     lon_odd = lax.rem(lon, 2) == 1
-    copies[0].wait()
-    copies[1].wait()
-    depth = (flag[...] * tally[...]).astype(jnp.float32)
-    depth_out[...] = depth
     lane = lanes_of((ROWS, LANES))
     group = lane >> 3
     pair = (lane & 7) >> 1
     west = jnp.zeros((ROWS, LANES), jnp.float32)
     east = west
     for f, field in enumerate(fields):
+        copies[f].wait()
         acc = jnp.zeros((ROWS, LANES), jnp.float32)
         for k in range(LEVELS):
-            if k % (LEVELS // FETCHES) == 0:
-                copies[2 + f * FETCHES + k // (LEVELS // FETCHES)].wait()
             acc = jnp.where(group == k, shift(field[k], 8 * k + 2), acc)
         packed[f] = acc
         west = jnp.where(pair == f, shift(acc, 2 * f - 2), west)
         east = jnp.where(pair == f, shift(acc, 2 * f), east)
+    copies[4].wait()
+    copies[5].wait()
+    depth = (flag[...] * tally[...]).astype(jnp.float32)
+    depth_out[...] = depth
     short = lanes_of((8, LANES)) >> 1
     depth_west = jnp.zeros((8, LANES), jnp.float32)
     depth_east = depth_west
@@ -167,9 +170,9 @@
 
 
 def relay_kernel(even_low, odd, even_up, col_far, to_far, to_far_edge):
-    _, lon = position()
+    lat, lon = position()
     lon_odd = lax.rem(lon, 2) == 1
-    info_even = jnp.where(is_upper(lon), even_up[128:136, :], even_low[128:136, :])
+    info_even = jnp.where(is_late_even(lat, lon), even_up[128:136, :], even_low[128:136, :])
     info_odd = odd[128:136, :]
     blank = jnp.zeros((4, LANES), jnp.float32)
 
@@ -190,7 +193,7 @@
     lat, lon = position()
     lon_odd = lax.rem(lon, 2) == 1
     at_top = lat == N_LAT - 1
-    even_info = jnp.where(is_upper(lon), even_up[128:136, :], even_low[128:136, :])
+    even_info = jnp.where(is_late_even(lat, lon), even_up[128:136, :], even_low[128:136, :])
     odd_info = jnp.where(is_edge_run(lat), far_edge[176:184, :], odd[128:136, :])
 
     def beside(info, first):
@@ -338,7 +341,7 @@
     lon_odd = lax.rem(lon, 2) == 1
     fields = (heat, salt, zonal, merid)
     depth = depth_in[...]
-    even_rows = jnp.where(is_upper(lon), even_up[...], even_low[...])
+    even_rows = jnp.where(is_late_even(lat, lon), even_up[...], even_low[...])
     odd_rows = odd[...]
     south_rows = jnp.where(lat_odd, even_rows, odd_rows)
     north_rows = jnp.where(lat_odd, odd_rows, even_rows)
@@ -397,7 +400,7 @@
             part = reversed_lanes(odd_rows[at : min(at + 16, 130)])
             turned[at : min(at + 16, 130), :] = -part if at < 128 and at // 16 % 4 >= 2 else part
 
-    even_rows = jnp.where(is_upper(lon), even_up[...], even_low[...])
+    even_rows = jnp.where(is_late_even(lat, lon), even_up[...], even_low[...])
     even_beside = jnp.where(late, near_up[40:42, :], even_rows[132:134])
     beside = jnp.where(late, near_up[42:44, :], beside)
     odd_info = odd_rows[130:132]
@@ -612,15 +615,15 @@
         pack_kernel,
         [size] * 4 + [(ROWS, LANES), (4, ROWS, LANES), (8, LANES), (8, LANES), (40, LANES), (40, LANES)],
         *pinned,
-        scratch=[pltpu.VMEM((ROWS, LANES), jnp.int32)] * 2 + [pltpu.SemaphoreType.DMA((2 + 4 * FETCHES,))],
+        scratch=[pltpu.VMEM((ROWS, LANES), jnp.int32)] * 2 + [pltpu.SemaphoreType.DMA((6,))],
         held_in=False,
     )
     near = send(col_near, near_lon, lambda lat, lon: not upper(lon) or lat == N_LAT - 1)
     rows = call(row_kernel, [(128, LANES)] * 3, *fields)
     row_low, row_odd, row_up = call(join_kernel, [(ROW_MSG, LANES)] * 3, *rows, info_top, info_bottom, near)
-    even_low = send(row_low, even_lat, lambda lat, lon: not upper(lon))
+    even_low = send(row_low, even_lat, meets_even_early)
     odd = send(row_odd, odd_or_diagonal, lambda lat, lon: lat > 0)
-    even_up = send(row_up, even_lat, lambda lat, lon: upper(lon))
+    even_up = send(row_up, even_lat, lambda lat, lon: not meets_even_early(lat, lon))
     to_far, to_far_edge = call(
         relay_kernel, [(COL_MSG, LANES), (EDGE_MSG, LANES)], even_low, odd, even_up, col_far
     )

time: 41.6 us -> 40.8 us (0.981)
  starting transfers between devices: 28.8 us -> 27.7 us
    ppermute x7, starting transfers between devices: 28.8 us -> 27.7 us  [send(): return lax.ppermute(array, ('lat', 'lon'), pairs(where_to, member))]
where the time goes in v5:
time: 40.8 us; the launch traced here: 40.5 us
  starting transfers between devices  27.7 us (68%)
  Pallas kernels  6.98 us (17%)
  waiting for transfers between devices  4.63 us (11%)
  between operations  0.77 us (2%)
    ppermute x7, starting transfers between devices, send(): return lax.ppermute(array, ('lat', 'lon'), pairs(where_to, member))  27.7 us
    pallas_call x7, Pallas kernels, call(): pl.pallas_call(kernel, out_shape=shapes(*outputs), in_specs=[vmem if held...  6.98 us
    ppermute x7, waiting for transfers between devices, send(): return lax.ppermute(array, ('lat', 'lon'), pairs(where_to, member))  4.63 us
  transfers between devices with their start and end apart: 7, of which 3 were waited for; matrix products, arithmetic and copies ran while one was open for 1% of the time, Pallas kernels for 4%

profile of v5, /device:TPU:6, one launch (start us, length us, event | category | flops | bytes accessed | tf_op | source)
XLA Modules:
  0.0 40.5 jit_solution(11243248832113661956)
XLA Ops:
  0.6 1.9 %shard_map.102 = (f32[16,32,128]{2,1,0:T(8,128)S(1)}, f32[16,32,128]{2,1,0:T(8,128)S(1)}, f32[16,32,128]{2,1,0:T(8,128)S(1)}, f32[16,32,128]{2,1,0:T(8,128)S(1)}...) custom-call(f32[16,32,128]{2,1,0:T(8,128)} %heat_in.1, ...), custom_call_target="tpu_custom_call" | custom-call | tf_op jit(solution)/shard_map/pallas_call | solution.py:588
  2.5 1.9 %collective-permute-start = (f32[40,128]{1,0:T(8,128)S(1)}, f32[40,128]{1,0:T(8,128)S(1)}, u32[]{:S(2)}, u32[]{:S(2)}) collective-permute-start(f32[40,128]{1,0:T(8,128)S(1)} %get-tuple-element.33.col_near), channel_id=1, source_target_pairs={{0,1},{1,0},{4,5},{5,4},{8,9},{9,8},{12,13},{13,12},{16,17},{17,16... | collective-permute-start | bytes 61448 | tf_op jit(solution)/shard_map/ppermute | solution.py:64
  4.5 0.1 shard_map.103
  4.6 1.0 %collective-permute-done.near = f32[40,128]{1,0:T(8,128)S(1)} collective-permute-done((f32[40,128]{1,0:T(8,128)S(1)}, f32[40,128]{1,0:T(8,128)S(1)}, u32[]{:S(2)}, u32[]{:S(2)}) %collective-permute-start) | collective-permute-done | bytes 20512 | tf_op jit(solution)/shard_map/ppermute | solution.py:64
  5.6 0.1 shard_map.104
  5.7 3.8 %collective-permute-start.1 = (f32[136,128]{1,0:T(8,128)S(1)}, f32[136,128]{1,0:T(8,128)S(1)}, u32[]{:S(2)}, u32[]{:S(2)}) collective-permute-start(f32[136,128]{1,0:T(8,128)S(1)} %get-tuple-element.34), channel_id=1, source_target_pairs={{0,16},{1,17},{4,20},{5,21},{8,24},{9,25},{12,28},{13,29},{16,0},{... | collective-permute-start | bytes 208904 | tf_op jit(solution)/shard_map/ppermute | solution.py:64
  9.5 8.1 %collective-permute-start.2 = (f32[136,128]{1,0:T(8,128)S(1)}, f32[136,128]{1,0:T(8,128)S(1)}, u32[]{:S(2)}, u32[]{:S(2)}) collective-permute-start(f32[136,128]{1,0:T(8,128)S(1)} %get-tuple-element.35), channel_id=1, source_target_pairs={{16,32},{17,33},{18,34},{19,35},{20,36},{21,37},{22,38},{23,39},{2... | collective-permute-start | bytes 208904 | tf_op jit(solution)/shard_map/ppermute | solution.py:64
  17.7 0.7 %collective-permute-start.3 = (f32[136,128]{1,0:T(8,128)S(1)}, f32[136,128]{1,0:T(8,128)S(1)}, u32[]{:S(2)}, u32[]{:S(2)}) collective-permute-start(f32[136,128]{1,0:T(8,128)S(1)} %get-tuple-element.36), channel_id=1, source_target_pairs={{2,18},{3,19},{6,22},{7,23},{10,26},{11,27},{14,30},{15,31},{18,2}... | collective-permute-start | bytes 208904 | tf_op jit(solution)/shard_map/ppermute | solution.py:64
  18.3 0.0 collective-permute-done.1.even_low
  18.3 1.3 %collective-permute-done.2.odd = f32[136,128]{1,0:T(8,128)S(1)} collective-permute-done((f32[136,128]{1,0:T(8,128)S(1)}, f32[136,128]{1,0:T(8,128)S(1)}, u32[]{:S(2)}, u32[]{:S(2)}) %collective-permute-start.2) | collective-permute-done | bytes 69664 | tf_op jit(solution)/shard_map/ppermute | solution.py:64
  19.6 0.0 collective-permute-done.3.even_up
  19.7 0.0 copy-start
  19.7 11.9 %collective-permute-start.4 = (f32[184,128]{1,0:T(8,128)S(1)}, f32[184,128]{1,0:T(8,128)S(1)}, u32[]{:S(2)}, u32[]{:S(2)}) collective-permute-start(f32[184,128]{1,0:T(8,128)S(1)} %get-tuple-element.38), channel_id=1, source_target_pairs={{112,127},{113,114},{114,113},{115,116},{116,115},{117,118},{118,1... | collective-permute-start | bytes 282632 | tf_op jit(solution)/shard_map/ppermute | solution.py:64
  31.6 0.0 copy-done
  31.7 0.1 slice.14
  31.8 0.1 slice.15
  31.8 0.1 concatenate.7
  31.9 0.7 %collective-permute-start.6 = (f32[48,128]{1,0:T(8,128)S(1)}, f32[48,128]{1,0:T(8,128)S(1)}, u32[]{:S(2)}, u32[]{:S(2)}) collective-permute-start(f32[48,128]{1,0:T(8,128)S(1)} %get-tuple-element.39), channel_id=1, source_target_pairs={{0,15},{1,2},{2,1},{3,4},{4,3},{5,6},{6,5},{7,8},{8,7},{9,10},{10,... | collective-permute-start | bytes 73736 | tf_op jit(solution)/shard_map/ppermute | solution.py:64
  32.6 0.1 broadcast_in_dim.2.angles
  32.7 1.6 %shard_map.105._.mid = f32[4,16,32,128]{3,2,1,0:T(8,128)S(1)} custom-call(f32[16,32,128]{2,1,0:T(8,128)S(1)} %get-tuple-element.22.heat, f32[16,32,128]{2,1,0:T(8,128)S(1)} %get-tuple-element.23.salt, f32[16,32,128]{2,1,0:T(8,128)S(1)} %get-tuple-element.24.zonal, f32[16,32,128]{2,1,0:T(8,128)S(1)} %get-tuple-element.25.merid, ...), custom_call_target="tpu_custom_call" | custom-call | flops 30000000 | bytes 2097152 | tf_op jit(solution)/shard_map/pallas_call | solution.py:588
  34.2 2.3 %collective-permute-done.4.far_edge = f32[184,128]{1,0:T(8,128)S(1)} collective-permute-done((f32[184,128]{1,0:T(8,128)S(1)}, f32[184,128]{1,0:T(8,128)S(1)}, u32[]{:S(2)}, u32[]{:S(2)}) %collective-permute-start.4) | collective-permute-done | bytes 94240 | tf_op jit(solution)/shard_map/ppermute | solution.py:64
  36.5 0.1 shard_map.107
  36.6 0.7 %collective-permute-start.5 = (f32[48,128]{1,0:T(8,128)S(1)}, f32[48,128]{1,0:T(8,128)S(1)}, u32[]{:S(2)}, u32[]{:S(2)}) collective-permute-start(f32[48,128]{1,0:T(8,128)S(1)} %shard_map.107), channel_id=1, source_target_pairs={{2,3},{3,2},{6,7},{7,6},{10,11},{11,10},{14,15},{15,14},{18,19},{1... | collective-permute-start | bytes 73736 | tf_op jit(solution)/shard_map/ppermute | solution.py:64
  37.3 0.0 collective-permute-done.6.far
  37.3 0.0 collective-permute-done.5.near_up
  37.3 3.2 %shard_map.108 = (f32[16,32,128]{2,1,0:T(8,128)}, f32[16,32,128]{2,1,0:T(8,128)}, f32[16,32,128]{2,1,0:T(8,128)}, f32[16,32,128]{2,1,0:T(8,128)}) custom-call(f32[4,16,32,128]{3,2,1,0:T(8,128)S(1)} %shard_map.105._.mid, f32[16,32,128]{2,1,0:T(8,128)S(1)} %get-tuple-element.22.heat, f32[16,32,128]{2,1,0:T(8,128)S(1)} %get-tuple-element.23.salt, ...), custom_call_target="tpu_custom_call" | custom-call | tf_op jit(solution)/shard_map/pallas_call | solution.py:588
  (4 shorter events, 0.1 us)
Async XLA Ops:
  2.5 3.1 %collective-permute-start = (f32[40,128]{1,0:T(8,128)S(1)}, f32[40,128]{1,0:T(8,128)S(1)}, u32[]{:S(2)}, u32[]{:S(2)}) collective-permute-start(f32[40,128]{1,0:T(8,128)S(1)} %get-tuple-element.33.col_near), channel_id=1, source_target_pairs={{0,1},{1,0},{4,5},{5,4},{8,9},{9,8},{12,13},{13,12},{16,17},{17,16... | collective-permute-start | bytes 61448 | tf_op jit(solution)/shard_map/ppermute | solution.py:64
  5.7 12.6 %collective-permute-start.1 = (f32[136,128]{1,0:T(8,128)S(1)}, f32[136,128]{1,0:T(8,128)S(1)}, u32[]{:S(2)}, u32[]{:S(2)}) collective-permute-start(f32[136,128]{1,0:T(8,128)S(1)} %get-tuple-element.34), channel_id=1, source_target_pairs={{0,16},{1,17},{4,20},{5,21},{8,24},{9,25},{12,28},{13,29},{16,0},{... | collective-permute-start | bytes 208904 | tf_op jit(solution)/shard_map/ppermute | solution.py:64
  9.5 10.1 %collective-permute-start.2 = (f32[136,128]{1,0:T(8,128)S(1)}, f32[136,128]{1,0:T(8,128)S(1)}, u32[]{:S(2)}, u32[]{:S(2)}) collective-permute-start(f32[136,128]{1,0:T(8,128)S(1)} %get-tuple-element.35), channel_id=1, source_target_pairs={{16,32},{17,33},{18,34},{19,35},{20,36},{21,37},{22,38},{23,39},{2... | collective-permute-start | bytes 208904 | tf_op jit(solution)/shard_map/ppermute | solution.py:64
  17.7 2.0 %collective-permute-start.3 = (f32[136,128]{1,0:T(8,128)S(1)}, f32[136,128]{1,0:T(8,128)S(1)}, u32[]{:S(2)}, u32[]{:S(2)}) collective-permute-start(f32[136,128]{1,0:T(8,128)S(1)} %get-tuple-element.36), channel_id=1, source_target_pairs={{2,18},{3,19},{6,22},{7,23},{10,26},{11,27},{14,30},{15,31},{18,2}... | collective-permute-start | bytes 208904 | tf_op jit(solution)/shard_map/ppermute | solution.py:64
  19.7 11.9 %copy-start = (s32[34]{0:T(128)S(1)}, s32[34]{0:T(128)}, u32[]{:S(2)}) copy-start(s32[34]{0:T(128)} %constant.29) | copy-start | bytes 412
  19.7 16.9 %collective-permute-start.4 = (f32[184,128]{1,0:T(8,128)S(1)}, f32[184,128]{1,0:T(8,128)S(1)}, u32[]{:S(2)}, u32[]{:S(2)}) collective-permute-start(f32[184,128]{1,0:T(8,128)S(1)} %get-tuple-element.38), channel_id=1, source_target_pairs={{112,127},{113,114},{114,113},{115,116},{116,115},{117,118},{118,1... | collective-permute-start | bytes 282632 | tf_op jit(solution)/shard_map/ppermute | solution.py:64
  31.9 5.4 %collective-permute-start.6 = (f32[48,128]{1,0:T(8,128)S(1)}, f32[48,128]{1,0:T(8,128)S(1)}, u32[]{:S(2)}, u32[]{:S(2)}) collective-permute-start(f32[48,128]{1,0:T(8,128)S(1)} %get-tuple-element.39), channel_id=1, source_target_pairs={{0,15},{1,2},{2,1},{3,4},{4,3},{5,6},{6,5},{7,8},{8,7},{9,10},{10,... | collective-permute-start | bytes 73736 | tf_op jit(solution)/shard_map/ppermute | solution.py:64
  36.6 0.7 %collective-permute-start.5 = (f32[48,128]{1,0:T(8,128)S(1)}, f32[48,128]{1,0:T(8,128)S(1)}, u32[]{:S(2)}, u32[]{:S(2)}) collective-permute-start(f32[48,128]{1,0:T(8,128)S(1)} %shard_map.107), channel_id=1, source_target_pairs={{2,3},{3,2},{6,7},{7,6},{10,11},{11,10},{14,15},{15,14},{18,19},{1... | collective-permute-start | bytes 73736 | tf_op jit(solution)/shard_map/ppermute | solution.py:64
